TPU v7x, 128 devices: a whole 4x4x4 slice. The times are simulated.
128 devices in a mesh: clip: 64 (over y, z_lo, x, core), frame: 2 (over z_hi).
Axes of the slice: x: 4, y: 4, z: 4 (z_hi: 2, z_lo: 2; z = z_hi * 2 + z_lo), core: 2. Of those that a mesh axis runs over, the one named last changes fastest.
Arguments:
- tokens: bfloat16 [64, 8, 324, 384], P('clip', 'frame'), may hold values from -6 to 6
- attn_gain: float32 [384], replicated, may hold values from 0.25 to 1.75
- attn_shift: float32 [384], replicated, may hold values from -3 to 3
- w_qkv: bfloat16 [384, 1152], replicated, may hold values from -0.3125 to 0.3125
- query_bias: bfloat16 [384], replicated, may hold values from -4 to 4
- value_bias: bfloat16 [384], replicated, may hold values from -4 to 4
- w_proj: bfloat16 [384, 384], replicated, may hold values from -2.5 to 2.5
- proj_bias: bfloat16 [384], replicated, may hold values from -4 to 4
- mlp_gain: float32 [384], replicated, may hold values from 0.25 to 1.75
- mlp_shift: float32 [384], replicated, may hold values from -3 to 3
- w_expand: bfloat16 [384, 1536], replicated, may hold values from -0.3125 to 0.3125
- expand_bias: bfloat16 [1536], replicated, may hold values from -4 to 4
- w_reduce: bfloat16 [1536, 384], replicated, may hold values from -0.15625 to 0.15625
- reduce_bias: bfloat16 [384], replicated, may hold values from -4 to 4
- cotangent: bfloat16 [64, 8, 324, 384], P('clip', 'frame'), may hold values from -6 to 6
- resolution: int32 [64], P('clip'), may hold values from 100 to 324, as said below
- frame_count: int32 [64], P('clip'), may hold values from 5 to 8, as said below
Outputs:
- activations: bfloat16 [64, 8, 324, 384], P('clip', 'frame')
- grad_tokens: float32 [64, 8, 324, 384], P('clip', 'frame')
- grad_attn_gain: float32 [384], replicated
- grad_attn_shift: float32 [384], replicated
- grad_w_qkv: float32 [384, 1152], replicated
- grad_query_bias: float32 [384], replicated
- grad_value_bias: float32 [384], replicated
- grad_w_proj: float32 [384, 384], replicated
- grad_proj_bias: float32 [384], replicated
- grad_mlp_gain: float32 [384], replicated
- grad_mlp_shift: float32 [384], replicated
- grad_w_expand: float32 [384, 1536], replicated
- grad_expand_bias: float32 [1536], replicated
- grad_w_reduce: float32 [1536, 384], replicated
- grad_reduce_bias: float32 [384], replicated
- grad_norm: float32 [], replicated
Inputs may be any that keep to these rules, and one draw needn't show every extreme that they name: `resolution`: each clip's value is one of 324 * 100 // 324, 324 * 196 // 324 and 324; some clip has 324. `frame_count`: some clip has all 8 frames live.
All inputs are finite; a program needn't handle non-finite values.
Results may differ from a plain program's by a relative error of at most 0.012.
Values may be sent and summed in bfloat16 or wider, within the bound.
A program may use at most 256 MiB of HBM per device.

v0:
```python
import jax
import jax.numpy as jnp
from jax import lax
from jax.sharding import PartitionSpec as P

HEADS = 6


EPS = 1e-06
SCALE = 0.125


def with_halo(value, sides, width):
    for axis, dim in sides:
        count, length = (lax.axis_size(axis), value.shape[dim])
        up = [(i, (i + 1) % count) for i in range(count - 1)]
        down = [(j, i) for i, j in up]
        last = lax.slice_in_dim(value, length - width, length, axis=dim)
        first = lax.slice_in_dim(value, 0, width, axis=dim)
        before = lax.ppermute(last, axis, up)
        after = lax.ppermute(first, axis, down)
        value = jnp.concatenate([before, value, after], axis=dim)
    return value


def from_behind(value, axis, steps):
    count = lax.axis_size(axis)
    first, last = (max(0, -steps), min(count, count - steps))
    return lax.ppermute(value, axis, [(source, source + steps) for source in range(first, last)])


def norm_forward(values, scale_vector, shift_vector):
    centre = values - jnp.mean(values, axis=-1, keepdims=True)
    spread = jnp.mean(centre * centre, axis=-1, keepdims=True)
    inverse = lax.rsqrt(spread + EPS)
    scaled = centre * inverse
    return (scaled * scale_vector + shift_vector, scaled, inverse)


def norm_backward(grad_out, scaled, inverse, scale_vector):
    weighted = grad_out * scale_vector
    return inverse * (
        weighted
        - jnp.mean(weighted, axis=-1, keepdims=True)
        - scaled * jnp.mean(weighted * scaled, axis=-1, keepdims=True)
    )


def inner_product(first_operand, second_operand):
    return lax.dot_general(
        first_operand, second_operand, (((0,), (0,)), ((), ())), preferred_element_type=jnp.float32
    )


def times_transpose(operand, matrix):
    return lax.dot_general(
        operand, matrix, (((1,), (1,)), ((), ())), preferred_element_type=jnp.float32
    )


def exact_gelu(values):
    return jax.nn.gelu(values, approximate=False)


def windows(extended, frames_here):
    return jnp.concatenate([extended[offset : offset + frames_here] for offset in range(3)], axis=1)


def unwindow(windowed):
    positions = windowed.shape[1] // 3
    pieces = [windowed[:, offset * positions : (offset + 1) * positions] for offset in range(3)]
    trailing = ((0, 0),) * (windowed.ndim - 1)
    result = jnp.pad(pieces[0], ((0, 2),) + trailing)
    result = result + jnp.pad(pieces[1], ((1, 1),) + trailing)
    return result + jnp.pad(pieces[2], ((2, 0),) + trailing)


def split_heads(blocked, features):
    return blocked.reshape(blocked.shape[0], blocked.shape[1], HEADS, features // HEADS)


def scores_for(query_block, extended, visible_ext):
    frames_here = query_block.shape[0]
    features = query_block.shape[-1]
    kv_windows = windows(extended, frames_here)
    key_heads = split_heads(kv_windows[..., :features], features)
    value_heads = split_heads(kv_windows[..., features:], features)
    query_heads = split_heads(query_block, features)
    visible = windows(visible_ext, frames_here)
    products = (
        jnp.einsum("fqhd,fkhd->fhqk", query_heads, key_heads, preferred_element_type=jnp.float32)
        * SCALE
    )
    scores = jnp.where(visible[:, None, None, :] > 0, products, -1000000000.0)
    return (scores, query_heads, key_heads, value_heads)


def attend(inputs):
    query_block, extended, visible_ext = inputs
    scores, query_heads, key_heads, value_heads = scores_for(query_block, extended, visible_ext)
    largest = jnp.max(scores, axis=-1, keepdims=True)
    exponent = jnp.exp(scores - largest)
    denominator = jnp.sum(exponent, axis=-1, keepdims=True)
    weights = (exponent / denominator).astype(jnp.bfloat16)
    blended = jnp.einsum(
        "fhqk,fkhd->fqhd", weights, value_heads, preferred_element_type=jnp.float32
    )
    return (blended.reshape(query_block.shape), (largest + jnp.log(denominator))[..., 0])


def attend_back(inputs):
    query_block, extended, visible_ext, log_totals, grad_blended = inputs
    features = query_block.shape[-1]
    scores, query_heads, key_heads, value_heads = scores_for(query_block, extended, visible_ext)
    weights = jnp.exp(scores - log_totals[..., None])
    weights_low = weights.astype(jnp.bfloat16)
    grad_heads = split_heads(grad_blended, features)
    grad_weights = jnp.einsum(
        "fqhd,fkhd->fhqk", grad_heads, value_heads, preferred_element_type=jnp.float32
    )
    centred = jnp.sum(weights * grad_weights, axis=-1, keepdims=True)
    grad_scores = (weights * (grad_weights - centred)).astype(jnp.bfloat16)
    grad_query = (
        jnp.einsum("fhqk,fkhd->fqhd", grad_scores, key_heads, preferred_element_type=jnp.float32)
        * SCALE
    )
    grad_keys = (
        jnp.einsum("fhqk,fqhd->fkhd", grad_scores, query_heads, preferred_element_type=jnp.float32)
        * SCALE
    )
    grad_values = jnp.einsum(
        "fhqk,fqhd->fkhd", weights_low, grad_heads, preferred_element_type=jnp.float32
    )
    frames_here, window_rows = grad_keys.shape[:2]
    paired = jnp.concatenate(
        [
            grad_keys.reshape(frames_here, window_rows, features),
            grad_values.reshape(frames_here, window_rows, features),
        ],
        axis=-1,
    )
    return (grad_query.reshape(query_block.shape), unwindow(paired))


def body(
    tokens,
    attn_gain,
    attn_shift,
    w_qkv,
    query_bias,
    value_bias,
    w_proj,
    proj_bias,
    mlp_gain,
    mlp_shift,
    w_expand,
    expand_bias,
    w_reduce,
    reduce_bias,
    cotangent,
    resolution,
    frame_count,
):
    clips_here, frames_here, positions, features = tokens.shape
    row_count = clips_here * frames_here * positions
    first_frame = lax.axis_index("frame") * frames_here
    position_ids = jnp.arange(positions)
    own_frames = first_frame + jnp.arange(frames_here)
    rim_frames = first_frame - 1 + jnp.arange(frames_here + 2)
    position_live = position_ids[None, None, :] < resolution[:, None, None]
    live = (position_live & (own_frames[None, :, None] < frame_count[:, None, None])).astype(
        jnp.float32
    )
    visible_ext = (
        position_live
        & (rim_frames[None, :, None] >= 0)
        & (rim_frames[None, :, None] < frame_count[:, None, None])
    ).astype(jnp.float32)
    flattened = tokens.astype(jnp.float32).reshape(row_count, features)
    normed, scaled_one, inverse_one = norm_forward(flattened, attn_gain, attn_shift)
    normed_low = normed.astype(jnp.bfloat16)
    joined = jnp.dot(normed_low, w_qkv, preferred_element_type=jnp.float32)
    queries = (joined[:, :features] + query_bias.astype(jnp.float32)).astype(jnp.bfloat16)
    key_rows = joined[:, features : 2 * features].astype(jnp.bfloat16)
    value_rows = (joined[:, 2 * features :] + value_bias.astype(jnp.float32)).astype(jnp.bfloat16)
    paired = jnp.concatenate([key_rows, value_rows], axis=-1).reshape(
        clips_here, frames_here, positions, 2 * features
    )
    extended = with_halo(paired, (("frame", 1),), 1)
    query_blocks = queries.reshape(clips_here, frames_here, positions, features)
    blended, log_totals = lax.map(attend, (query_blocks, extended, visible_ext))
    blended_low = blended.reshape(row_count, features).astype(jnp.bfloat16)
    hidden = (
        flattened
        + jnp.dot(blended_low, w_proj, preferred_element_type=jnp.float32)
        + proj_bias.astype(jnp.float32)
    )
    second, scaled_two, inverse_two = norm_forward(hidden, mlp_gain, mlp_shift)
    second_low = second.astype(jnp.bfloat16)
    expanded = jnp.dot(
        second_low, w_expand, preferred_element_type=jnp.float32
    ) + expand_bias.astype(jnp.float32)
    activated, gelu_pullback = jax.vjp(exact_gelu, expanded)
    activated_low = activated.astype(jnp.bfloat16)
    output = (
        hidden
        + jnp.dot(activated_low, w_reduce, preferred_element_type=jnp.float32)
        + reduce_bias.astype(jnp.float32)
    )
    activations = output.astype(jnp.bfloat16).reshape(tokens.shape)
    upstream = cotangent.astype(jnp.float32).reshape(row_count, features) * live.reshape(
        row_count, 1
    )
    upstream_low = upstream.astype(jnp.bfloat16)
    grad_w_reduce = inner_product(activated_low, upstream_low)
    grad_reduce_bias = jnp.sum(upstream, axis=0)
    grad_expanded = gelu_pullback(times_transpose(upstream_low, w_reduce))[0].astype(jnp.bfloat16)
    grad_w_expand = inner_product(second_low, grad_expanded)
    grad_expand_bias = jnp.sum(grad_expanded.astype(jnp.float32), axis=0)
    grad_second = times_transpose(grad_expanded, w_expand)
    grad_mlp_gain = jnp.sum(grad_second * scaled_two, axis=0)
    grad_mlp_shift = jnp.sum(grad_second, axis=0)
    grad_hidden = upstream + norm_backward(grad_second, scaled_two, inverse_two, mlp_gain)
    grad_branch = grad_hidden.astype(jnp.bfloat16)
    grad_w_proj = inner_product(blended_low, grad_branch)
    grad_proj_bias = jnp.sum(grad_branch.astype(jnp.float32), axis=0)
    grad_blended = (
        times_transpose(grad_branch, w_proj)
        .astype(jnp.bfloat16)
        .reshape(clips_here, frames_here, positions, features)
    )
    grad_queries, grad_rims = lax.map(
        attend_back, (query_blocks, extended, visible_ext, log_totals, grad_blended)
    )
    from_next = from_behind(grad_rims[:, :1].astype(jnp.bfloat16), "frame", -1).astype(jnp.float32)
    from_prev = from_behind(
        grad_rims[:, frames_here + 1 :].astype(jnp.bfloat16), "frame", 1
    ).astype(jnp.float32)
    grad_paired = (
        grad_rims[:, 1 : frames_here + 1]
        + jnp.pad(from_prev, ((0, 0), (0, frames_here - 1), (0, 0), (0, 0)))
        + jnp.pad(from_next, ((0, 0), (frames_here - 1, 0), (0, 0), (0, 0)))
    )
    grad_joined = jnp.concatenate(
        [grad_queries.reshape(row_count, features), grad_paired.reshape(row_count, 2 * features)],
        axis=-1,
    ).astype(jnp.bfloat16)
    grad_w_qkv = inner_product(normed_low, grad_joined)
    grad_query_bias = jnp.sum(grad_joined[:, :features].astype(jnp.float32), axis=0)
    grad_value_bias = jnp.sum(grad_joined[:, 2 * features :].astype(jnp.float32), axis=0)
    grad_normed = times_transpose(grad_joined, w_qkv)
    grad_attn_gain = jnp.sum(grad_normed * scaled_one, axis=0)
    grad_attn_shift = jnp.sum(grad_normed, axis=0)
    grad_tokens = (
        grad_hidden + norm_backward(grad_normed, scaled_one, inverse_one, attn_gain)
    ).reshape(tokens.shape)
    (
        grad_attn_gain,
        grad_attn_shift,
        grad_w_qkv,
        grad_query_bias,
        grad_value_bias,
        grad_w_proj,
        grad_proj_bias,
        grad_mlp_gain,
        grad_mlp_shift,
        grad_w_expand,
        grad_expand_bias,
        grad_w_reduce,
        grad_reduce_bias,
    ) = lax.psum(
        (
            grad_attn_gain,
            grad_attn_shift,
            grad_w_qkv,
            grad_query_bias,
            grad_value_bias,
            grad_w_proj,
            grad_proj_bias,
            grad_mlp_gain,
            grad_mlp_shift,
            grad_w_expand,
            grad_expand_bias,
            grad_w_reduce,
            grad_reduce_bias,
        ),
        ("clip", "frame"),
    )
    squares = jnp.float32(0.0)
    for gradient in (
        grad_attn_gain,
        grad_attn_shift,
        grad_w_qkv,
        grad_query_bias,
        grad_value_bias,
        grad_w_proj,
        grad_proj_bias,
        grad_mlp_gain,
        grad_mlp_shift,
        grad_w_expand,
        grad_expand_bias,
        grad_w_reduce,
        grad_reduce_bias,
    ):
        squares = squares + jnp.sum(gradient * gradient)
    grad_norm = jnp.sqrt(squares)
    return (
        activations,
        grad_tokens,
        grad_attn_gain,
        grad_attn_shift,
        grad_w_qkv,
        grad_query_bias,
        grad_value_bias,
        grad_w_proj,
        grad_proj_bias,
        grad_mlp_gain,
        grad_mlp_shift,
        grad_w_expand,
        grad_expand_bias,
        grad_w_reduce,
        grad_reduce_bias,
        grad_norm,
    )


def solution(mesh):
    return jax.shard_map(
        body,
        mesh=mesh,
        in_specs=(
            P("clip", "frame", None, None),
            P(),
            P(),
            P(),
            P(),
            P(),
            P(),
            P(),
            P(),
            P(),
            P(),
            P(),
            P(),
            P(),
            P("clip", "frame", None, None),
            P("clip"),
            P("clip"),
        ),
        out_specs=(
            P("clip", "frame", None, None),
            P("clip", "frame", None, None),
            P(),
            P(),
            P(),
            P(),
            P(),
            P(),
            P(),
            P(),
            P(),
            P(),
            P(),
            P(),
            P(),
            P(),
        ),
        check_vma=False,
    )
```

profile of v0, /device:TPU:1, one launch (start us, length us, event | category | flops | bytes accessed | tf_op | source)
XLA Modules:
  0.0 495.1 jit_solution(14926595626841652933)
XLA Ops:
  26.6 7.1 %collective-permute-start = (bf16[1,1,324,768]{3,2,1,0:T(8,128)(2,1)}, bf16[1,1,324,768]{3,2,1,0:T(8,128)(2,1)}, u32[]{:S(2)}, u32[]{:S(2)}) collective-permute-start(bf16[1,1,324,768]{3,2,1,0:T(8,128)(2,1)} %get-tuple-element.159), channel_id=1, source_target_pairs={{0,1},{2,3},{4,5},{6,7},{8,9},{10,11},{12,13},{14,15},{16,17},{18,... | collective-permute-start | bytes 1493000 | tf_op jit(solution)/shard_map/ppermute | solution.py:20
  62.3 4.6 copy.88
  66.9 4.6 copy.86
  71.5 15.1 %fusion.6 = (f32[4,6,324]{2,1,0:T(8,128)S(1)}, f32[4,6,324,972]{3,2,1,0:T(8,128)}) fusion(pred[4,972]{1,0:T(4,128)(4,1)S(1)} %maximum_compare_fusion, bf16[4,972,6,64]{1,3,2,0:T(8,128)(2,1)} %bitcast.62, bf16[4,324,6,64]{1,0,3,2:T(4,128)(2,1)} %reshape.365), kind=kOutput, calls=%fused_computation.15 | convolution fusion | flops 990125824 | bytes 34249392 | tf_op jit(solution)/shard_map/while/body/eval_jaxpr/fqhd,fkhd->fhqk/dot_general | solution.py:91
  86.7 14.4 %fusion = f32[4,6,324]{2,1,0:T(8,128)S(1)} fusion(f32[4,6,324]{2,1,0:T(8,128)S(1)} %get-tuple-element.164, f32[4,6,324,972]{3,2,1,0:T(8,128)} %get-tuple-element.165, pred[4,972]{1,0:T(4,128)(4,1)S(1)} %maximum_compare_fusion), kind=kLoop, calls=%fused_computation.6 | loop fusion | flops 30225312 | bytes 30299184 | tf_op jit(solution)/shard_map/while/body/eval_jaxpr/reduce_sum | solution.py:103
  101.2 13.3 %fusion.30 = bf16[4,324,6,64]{1,3,2,0:T(8,128)(2,1)S(1)} fusion(bf16[4,972,6,64]{1,3,2,0:T(8,128)(2,1)S(1)} %bitcast.65, f32[4,6,324]{2,1,0:T(8,128)S(1)} %fusion, f32[4,6,324]{2,1,0:T(8,128)S(1)} %get-tuple-element.164, f32[4,6,324,972]{3,2,1,0:T(8,128)} %get-tuple-element.165, pred[4,972]{1,0:T(4,128)(4,1)S(1)} %maximum_compare_fusion), kind=kOutput, calls=%fused_computation.90 | convolution fusion | flops 1005747840 | bytes 34280496 | tf_op jit(solution)/shard_map/while/body/eval_jaxpr/fhqk,fkhd->fqhd/dot_general | solution.py:105
  122.8 20.9 %multiply_convert_fusion.1 = (bf16[1296,1536]{1,0:T(8,128)(2,1)}, f32[1296,1536]{1,0:T(8,128)S(1)}, f32[1296,1536]{1,0:T(8,128)}) fusion(f32[1536]{0:T(1024)S(1)} %convert_element_type.137, bf16[384,1536]{1,0:T(8,128)(2,1)S(1)} %copy-done, f32[1296,384]{1,0:T(8,128)S(1)} %get-tuple-element.167, f32[384]{0:T(512)S(1)} %copy-done.50, f32[384]{0:T(512)S(1)} %copy-done.34, ...), kind=kOutput, calls=%fused_computation.21 | convolution fusion | flops 1662695424 | bytes 23096448 | tf_op jit(solution)/shard_map/dot_general | solution.py:200
  143.8 7.7 %convert_reduce_fusion = (f32[1536]{0:T(1024)}, bf16[1296,1536]{1,0:T(8,128)(2,1)S(1)}) fusion(f32[1296,1536]{1,0:T(8,128)S(1)} %get-tuple-element.148, f32[1296,1536]{1,0:T(8,128)} %get-tuple-element.168, bf16[1536,384]{1,0:T(8,128)(2,1)S(1)} %copy-done.49, f32[1296,384]{1,0:T(8,128)S(1)} %copy-done.15, f32[1296]{0:T(1024)S(1)} %copy-done.25), kind=kOutput, calls=%fused_computation.19 | convolution fusion | flops 1561668096 | bytes 23088192 | tf_op jit(solution)/shard_map/dot_general | solution.py:56
  164.6 15.8 %fusion.2 = f32[4,6,64,972]{3,2,1,0:T(8,128)} fusion(f32[4,6,324]{2,1,0:T(8,128)S(1)} %log_add_fusion, f32[4,6,324,972]{3,2,1,0:T(8,128)} %get-tuple-element.165, pred[4,972]{1,0:T(4,128)(4,1)S(1)} %maximum_compare_fusion, bf16[4,324,6,64]{1,0,3,2:T(4,128)(2,1)S(1)} %reshape.369), kind=kOutput, calls=%fused_computation.8 | convolution fusion | flops 997691904 | bytes 37235376 | tf_op jit(solution)/shard_map/while/body/eval_jaxpr/fhqk,fqhd->fkhd/dot_general | solution.py:131
  180.4 22.9 %multiply_reduce_fusion = (f32[4,6,324]{2,1,0:T(8,128)S(1)}, f32[4,6,324,972]{3,2,1,0:T(8,128)}) fusion(f32[4,6,324]{2,1,0:T(8,128)S(1)} %log_add_fusion, f32[4,6,324,972]{3,2,1,0:T(8,128)} %get-tuple-element.165, pred[4,972]{1,0:T(4,128)(4,1)S(1)} %maximum_compare_fusion, bf16[4,972,6,64]{1,3,2,0:T(8,128)(2,1)S(1)} %bitcast.66, ...), kind=kOutput, calls=%fused_computation.1 | convolution fusion | flops 1005242368 | bytes 64513584 | tf_op jit(solution)/shard_map/while/body/eval_jaxpr/fqhd,fkhd->fhqk/dot_general | solution.py:118
  203.3 26.6 %multiply_convert_fusion = bf16[4,6,324,972]{3,2,1,0:T(8,128)(2,1)} fusion(f32[4,6,324,972]{3,2,1,0:T(8,128)} %get-tuple-element.171, f32[4,6,324]{2,1,0:T(8,128)S(1)} %get-tuple-element.170, f32[4,6,324]{2,1,0:T(8,128)S(1)} %log_add_fusion, f32[4,6,324,972]{3,2,1,0:T(8,128)} %get-tuple-element.165, pred[4,972]{1,0:T(4,128)(4,1)S(1)} %maximum_compare_fusion), kind=kLoop, calls=%fused_computation | loop fusion | flops 45349632 | bytes 75648816 | tf_op jit(solution)/shard_map/while/body/eval_jaxpr/convert_element_type | solution.py:122
  229.9 9.2 %fusion.29 = bf16[4,324,6,64]{1,3,2,0:T(8,128)(2,1)S(1)} fusion(bf16[4,972,6,64]{1,3,2,0:T(8,128)(2,1)} %bitcast.63, bf16[4,6,324,972]{3,2,1,0:T(8,128)(2,1)} %multiply_convert_fusion), kind=kOutput, calls=%fused_computation.89 | convolution fusion | flops 968454144 | bytes 19097856 | tf_op jit(solution)/shard_map/while/body/eval_jaxpr/fhqk,fkhd->fqhd/dot_general | solution.py:124
  239.1 12.0 %broadcast_multiply_fusion = f32[4,6,64,972]{3,2,1,0:T(8,128)} fusion(bf16[4,6,324,972]{3,2,1,0:T(8,128)(2,1)} %multiply_convert_fusion, bf16[4,324,6,64]{1,0,3,2:T(4,128)(2,1)S(1)} %copy-done.9), kind=kOutput, calls=%fused_computation.45 | convolution fusion | flops 968951808 | bytes 22083840 | tf_op jit(solution)/shard_map/while/body/eval_jaxpr/fhqk,fqhd->fkhd/dot_general | solution.py:128
  251.1 6.4 %copy.98 = f32[4,972,384]{2,1,0:T(8,128)} copy(f32[4,972,384]{1,2,0:T(8,128)} %bitcast.67) | data formatting | bytes 11943936 | tf_op jit(solution)/shard_map/while/body/eval_jaxpr/reshape | solution.py:138
  257.6 6.5 %copy.97 = f32[4,972,384]{2,1,0:T(8,128)} copy(f32[4,972,384]{1,2,0:T(8,128)} %bitcast.64) | data formatting | bytes 11943936 | tf_op jit(solution)/shard_map/while/body/eval_jaxpr/reshape | solution.py:137
  267.3 3.8 fusion.16
  274.7 6.3 %collective-permute-start.2 = (bf16[1,1,324,768]{3,2,1,0:T(8,128)(2,1)S(1)}, bf16[1,1,324,768]{3,2,1,0:T(8,128)(2,1)S(1)}, u32[]{:S(2)}, u32[]{:S(2)}) collective-permute-start(bf16[1,1,324,768]{3,2,1,0:T(8,128)(2,1)S(1)} %get-tuple-element.155), channel_id=1, source_target_pairs={{0,1},{2,3},{4,5},{6,7},{8,9},{10,11},{12,13},{14,15},{16,17},{18,... | collective-permute-start | bytes 1493000 | tf_op jit(solution)/shard_map/ppermute | solution.py:29
  282.3 6.2 %fusion.48 = f32[1536,384]{1,0:T(8,128)} fusion(bf16[1296,1536]{1,0:T(8,128)(2,1)} %get-tuple-element.147, f32[1296,384]{1,0:T(8,128)S(1)} %copy-done.16, f32[1296]{0:T(1024)S(1)} %copy-done.25), kind=kOutput, calls=%fused_computation.138 | convolution fusion | flops 1529819136 | bytes 8336448 | tf_op jit(solution)/shard_map/dot_general | solution.py:50
  290.5 5.4 %collective-permute-done.3 = bf16[1,1,324,768]{3,2,1,0:T(8,128)(2,1)S(1)} collective-permute-done((bf16[1,1,324,768]{3,2,1,0:T(8,128)(2,1)S(1)}, bf16[1,1,324,768]{3,2,1,0:T(8,128)(2,1)S(1)}, u32[]{:S(2)}, u32[]{:S(2)}) %collective-permute-start.3) | collective-permute-done | bytes 497696 | tf_op jit(solution)/shard_map/ppermute | solution.py:29
  300.8 4.9 fusion.26
  306.4 6.3 %fusion.21 = bf16[1296,384]{1,0:T(8,128)(2,1)} fusion(f32[1296,384]{1,0:T(8,128)} %copy-done.6, bf16[1296,1536]{1,0:T(8,128)(2,1)} %get-tuple-element.147, bf16[1536,384]{1,0:T(8,128)(2,1)} %param.29, f32[384]{0:T(512)S(1)} %copy-done.44), kind=kOutput, calls=%fused_computation.51 | convolution fusion | flops 1530316800 | bytes 8148480 | tf_op jit(solution)/shard_map/dot_general | solution.py:207
  318.1 4.7 multiply_reduce_fusion.5
  328.8 67.4 %all-reduce.5 = (f32[384]{0:T(512)S(1)}, f32[384]{0:T(512)S(1)}, f32[384]{0:T(512)S(1)}, f32[384]{0:T(512)S(1)}, f32[384]{0:T(512)S(1)}, /*index=5*/f32[384]{0:T...) all-reduce(f32[384]{0:T(512)S(1)} %get-tuple-element.124, ...), channel_id=1, replica_groups=mesh['clip'=64,'frame'=2] {'clip','frame'}, use_global_device_ids=true, to_apply=%region_12.13 | all-reduce | flops 4608 | bytes 36864 | tf_op jit(solution)/shard_map/psum | solution.py:271
  403.3 63.8 %all-reduce.9.cloned.1.call-done = (f32[384,1152]{1,0:T(8,128)}, f32[384,384]{1,0:T(8,128)}, f32[384,1536]{1,0:T(8,128)}, f32[1536,384]{1,0:T(8,128)}) async-done(((f32[384,1152]{1,0:T(8,128)}, f32[384,384]{1,0:T(8,128)}, f32[384,1536]{1,0:T(8,128)}, f32[1536,384]{1,0:T(8,128)}), (f32[384,1152]{1,0:T(8,128)}, f32[384,384]{1,0:T(8,128)}, f32[384,1536]{1,0:T(8,128)}, ...) | async-done | bytes 7077904 | tf_op jit(solution)/shard_map/psum | solution.py:271
  (206 shorter events, 113.0 us)
Async XLA Ops:
  7.2 115.6 %copy-start = (bf16[384,1536]{1,0:T(8,128)(2,1)S(1)}, bf16[384,1536]{1,0:T(8,128)(2,1)}, u32[]{:S(2)}) copy-start(bf16[384,1536]{1,0:T(8,128)(2,1)} %param.27) | copy-start | bytes 3538948
  7.2 459.9 %all-reduce.9.cloned.1.call-start = ((), (), s32[]{:S(2)}) async-start(), calls=%async_computation | async-start | bytes 14155776 | tf_op jit(solution)/shard_map/psum | solution.py:271
  15.0 105.0 %copy-start.2 = (f32[1296,384]{1,0:T(8,128)}, f32[1296,384]{1,0:T(8,128)S(1)}, u32[]{:S(2)}) copy-start(f32[1296,384]{1,0:T(8,128)S(1)} %reshape.362) | copy-start | bytes 5971972
  24.4 15.4 %copy-start.47 = (bf16[384]{0:T(512)(128)(2,1)S(1)}, bf16[384]{0:T(512)(128)(2,1)}, u32[]{:S(2)}) copy-start(bf16[384]{0:T(512)(128)(2,1)} %param.24) | copy-start | bytes 2308
  24.4 15.4 %copy-start.48 = (bf16[384]{0:T(512)(128)(2,1)S(1)}, bf16[384]{0:T(512)(128)(2,1)}, u32[]{:S(2)}) copy-start(bf16[384]{0:T(512)(128)(2,1)} %param.30) | copy-start | bytes 2308
  24.4 16.0 %copy-start.33 = (bf16[1536]{0:T(1024)(128)(2,1)S(1)}, bf16[1536]{0:T(1024)(128)(2,1)}, u32[]{:S(2)}) copy-start(bf16[1536]{0:T(1024)(128)(2,1)} %param.28) | copy-start | bytes 9220
  26.6 28.7 %collective-permute-start = (bf16[1,1,324,768]{3,2,1,0:T(8,128)(2,1)}, bf16[1,1,324,768]{3,2,1,0:T(8,128)(2,1)}, u32[]{:S(2)}, u32[]{:S(2)}) collective-permute-start(bf16[1,1,324,768]{3,2,1,0:T(8,128)(2,1)} %get-tuple-element.159), channel_id=1, source_target_pairs={{0,1},{2,3},{4,5},{6,7},{8,9},{10,11},{12,13},{14,15},{16,17},{18,... | collective-permute-start | bytes 1493000 | tf_op jit(solution)/shard_map/ppermute | solution.py:20
  33.7 21.6 %collective-permute-start.1 = (bf16[1,1,324,768]{3,2,1,0:T(8,128)(2,1)}, bf16[1,1,324,768]{3,2,1,0:T(8,128)(2,1)}, u32[]{:S(2)}, u32[]{:S(2)}) collective-permute-start(bf16[1,1,324,768]{3,2,1,0:T(8,128)(2,1)} %get-tuple-element.160), channel_id=1, source_target_pairs={{1,0},{3,2},{5,4},{7,6},{9,8},{11,10},{13,12},{15,14},{17,16},{19,... | collective-permute-start | bytes 1493000 | tf_op jit(solution)/shard_map/ppermute | solution.py:21
  122.2 36.0 %copy-start.6 = (f32[1296,384]{1,0:T(8,128)}, f32[1296,384]{1,0:T(8,128)S(1)}, u32[]{:S(2)}) copy-start(f32[1296,384]{1,0:T(8,128)S(1)} %get-tuple-element.167) | copy-start | bytes 5971972
  122.8 21.0 %copy-start.15 = (f32[1296,384]{1,0:T(8,128)S(1)}, f32[1296,384]{1,0:T(8,128)}, u32[]{:S(2)}) copy-start(f32[1296,384]{1,0:T(8,128)} %reshape.368) | copy-start | bytes 5971972
  122.8 21.0 %copy-start.25 = (f32[1296]{0:T(1024)S(1)}, f32[1296]{0:T(1024)}, u32[]{:S(2)}) copy-start(f32[1296]{0:T(1024)} %and_convert_fusion.1) | copy-start | bytes 15556
  122.8 20.9 %copy-start.49 = (bf16[1536,384]{1,0:T(8,128)(2,1)S(1)}, bf16[1536,384]{1,0:T(8,128)(2,1)}, u32[]{:S(2)}) copy-start(bf16[1536,384]{1,0:T(8,128)(2,1)} %param.29) | copy-start | bytes 3538948
  164.6 15.8 %copy-start.8 = (bf16[4,972,384]{1,2,0:T(8,128)(2,1)S(1)}, bf16[4,972,384]{1,2,0:T(8,128)(2,1)}, u32[]{:S(2)}) copy-start(bf16[4,972,384]{1,2,0:T(8,128)(2,1)} %copy.86) | copy-start | bytes 8957956
  274.7 15.8 %collective-permute-start.2 = (bf16[1,1,324,768]{3,2,1,0:T(8,128)(2,1)S(1)}, bf16[1,1,324,768]{3,2,1,0:T(8,128)(2,1)S(1)}, u32[]{:S(2)}, u32[]{:S(2)}) collective-permute-start(bf16[1,1,324,768]{3,2,1,0:T(8,128)(2,1)S(1)} %get-tuple-element.155), channel_id=1, source_target_pairs={{0,1},{2,3},{4,5},{6,7},{8,9},{10,11},{12,13},{14,15},{16,17},{18,... | collective-permute-start | bytes 1493000 | tf_op jit(solution)/shard_map/ppermute | solution.py:29
  281.0 14.9 %collective-permute-start.3 = (bf16[1,1,324,768]{3,2,1,0:T(8,128)(2,1)S(1)}, bf16[1,1,324,768]{3,2,1,0:T(8,128)(2,1)S(1)}, u32[]{:S(2)}, u32[]{:S(2)}) collective-permute-start(bf16[1,1,324,768]{3,2,1,0:T(8,128)(2,1)S(1)} %get-tuple-element.156), channel_id=1, source_target_pairs={{1,0},{3,2},{5,4},{7,6},{9,8},{11,10},{13,12},{15,14},{17,16},{19,... | collective-permute-start | bytes 1493000 | tf_op jit(solution)/shard_map/ppermute | solution.py:29
  396.2 77.0 %copy-start.32 = (f32[1536]{0:T(1024)}, f32[1536]{0:T(1024)S(1)}, u32[]{:S(2)}) copy-start(f32[1536]{0:T(1024)S(1)} %get-tuple-element.189) | copy-start | bytes 18436
  396.2 77.0 %copy-start.36 = (f32[384]{0:T(512)}, f32[384]{0:T(512)S(1)}, u32[]{:S(2)}) copy-start(f32[384]{0:T(512)S(1)} %get-tuple-element.179) | copy-start | bytes 4612
  396.2 77.0 %copy-start.37 = (f32[384]{0:T(512)}, f32[384]{0:T(512)S(1)}, u32[]{:S(2)}) copy-start(f32[384]{0:T(512)S(1)} %get-tuple-element.180) | copy-start | bytes 4612
  396.2 77.0 %copy-start.38 = (f32[384]{0:T(512)}, f32[384]{0:T(512)S(1)}, u32[]{:S(2)}) copy-start(f32[384]{0:T(512)S(1)} %get-tuple-element.182) | copy-start | bytes 4612
  396.2 77.0 %copy-start.39 = (f32[384]{0:T(512)}, f32[384]{0:T(512)S(1)}, u32[]{:S(2)}) copy-start(f32[384]{0:T(512)S(1)} %get-tuple-element.183) | copy-start | bytes 4612
  396.2 77.0 %copy-start.40 = (f32[384]{0:T(512)}, f32[384]{0:T(512)S(1)}, u32[]{:S(2)}) copy-start(f32[384]{0:T(512)S(1)} %get-tuple-element.185) | copy-start | bytes 4612
  396.2 77.0 %copy-start.41 = (f32[384]{0:T(512)}, f32[384]{0:T(512)S(1)}, u32[]{:S(2)}) copy-start(f32[384]{0:T(512)S(1)} %get-tuple-element.186) | copy-start | bytes 4612
  396.2 77.0 %copy-start.42 = (f32[384]{0:T(512)}, f32[384]{0:T(512)S(1)}, u32[]{:S(2)}) copy-start(f32[384]{0:T(512)S(1)} %get-tuple-element.187) | copy-start | bytes 4612
  396.2 77.0 %copy-start.43 = (f32[384]{0:T(512)}, f32[384]{0:T(512)S(1)}, u32[]{:S(2)}) copy-start(f32[384]{0:T(512)S(1)} %get-tuple-element.191) | copy-start | bytes 4612
  (34 other events, 141.7 us)
Sparse Core Ops, SparseCore 0:
  305.9 161.1 all-reduce.8
where the time goes:
time: 501 us; the launch traced here: 495 us
  matrix products  154 us (31%)
  local copies, waits for them, and re-layouts  80.2 us (16%)
  other arithmetic  79.7 us (16%)
  waiting for transfers between devices  71.2 us (14%)
  blocking collectives  67.4 us (13%)
  between operations  26 us (5%)
  starting transfers between devices  16.2 us (3%)
    psum x1, blocking collectives, body(): lax.psum((grad_attn_gain, grad_attn_shift, grad_w_qkv, grad_query_bias, g...  67.4 us
    psum x1, waiting for transfers between devices, body(): lax.psum((grad_attn_gain, grad_attn_shift, grad_w_qkv, grad_query_bias, g...  63.8 us
    convert_element_type x1, other arithmetic, attend_back(): grad_scores = (weights * (grad_weights - centred)).astype(jnp.bfloat16)  26.6 us
    dot_general x1, matrix products, attend_back(): jnp.einsum('fqhd,fkhd->fhqk', grad_heads, value_heads, preferred_element_...  22.9 us
    dot_general x1, matrix products, body(): jnp.dot(second_low, w_expand, preferred_element_type=jnp.float32)  20.9 us
    dot_general x4, matrix products, times_transpose(): lax.dot_general(operand, matrix, (((1,), (1,)), ((), ())), preferred_elem...  16.5 us
    dot_general x4, matrix products, inner_product(): lax.dot_general(first_operand, second_operand, (((0,), (0,)), ((), ())),...  16.2 us
    dot_general x1, matrix products, attend_back(): jnp.einsum('fhqk,fqhd->fkhd', weights_low, grad_heads, preferred_element_...  15.8 us
  transfers between devices with their start and end apart: 5, of which 3 were waited for; matrix products, arithmetic and copies ran while one was open for 11% of the time, Pallas kernels for 0%

commit v1 on v0

v1 whole, which is shorter than its diff:
```python
import functools
import jax
import jax.numpy as jnp
from jax import lax
from jax.sharding import PartitionSpec as P
from jax.experimental import pallas as pl
from jax.experimental.pallas import tpu as pltpu

T = 324
F = 336
D = 384
FF = 1536
N = 4
PAIRS = 3
EPS = 1e-6
NEG = -1e9
PAD = -1e30
LANES = 128
CHUNK = 512
f32 = jnp.float32
bf16 = jnp.bfloat16
NT = (((1,), (1,)), ((), ()))
NN = (((1,), (0,)), ((), ()))
TN = (((0,), (0,)), ((), ()))
MESH = pl.DeviceIdType.MESH


def dot(a, b, dims=NN):
    return lax.dot_general(a, b, dims, preferred_element_type=f32)


def rows_of(slot):
    return pl.ds(pl.multiple_of(slot * F, 16), F)


def live_rows_of(slot):
    return pl.ds(pl.multiple_of(slot * F, 16), T)


def normalise(x):
    centre = x - jnp.mean(x, axis=1, keepdims=True)
    spread = jnp.mean(centre * centre, axis=1, keepdims=True)
    inverse = lax.rsqrt(spread + EPS)
    return centre * inverse, inverse


def norm_back(grad, scaled, inverse, gain):
    e = grad * gain
    return inverse * (
        e - jnp.mean(e, axis=1, keepdims=True) - scaled * jnp.mean(e * scaled, axis=1, keepdims=True)
    )


def gelu_parts(x):
    u = jnp.exp(-0.5 * (x * x))
    t = 1.0 / (1.0 + 0.23164188844 * jnp.abs(x))
    p = t * (0.127414796 + t * (-0.142248368 + t * (0.7107068705 + t * (-0.7265760135 + t * 0.5307027145))))
    h = p * u
    cdf = jnp.where(x >= 0, 1.0 - h, h)
    return x * cdf, cdf + x * (u * 0.3989422804014327)


def column_sum(x):
    return jnp.sum(x, axis=0, keepdims=True)
EARLY = 10752
LATE = 3840


def main_kernel(
    tokens, cot, w_qkv, w_proj, w_expand, w_reduce, vec_d, vec_ff, res, cnt,
    act_out, grad_out, early_out, late_out,
    x, up0, wq, wp, we, wr, n, q, k, v, e0, e, bl, inv, hid, sec, up, a, ge, gh, gb, gbl, gj,
    hsend, hrecv, ostage, gstage, early, late, acc_d, acc_ff, lsem, osem, hsem,
):
    z = lax.axis_index("frame")
    other = 1 - z

    def place(s):
        return s + z * (3 - 2 * s)

    local = []

    def fetch(src, dst):
        c = pltpu.make_async_copy(src, dst, lsem.at[len(local)])
        c.start()
        local.append(c)
        return c

    cx = [fetch(tokens.at[0, place(s)], x.at[s]) for s in range(N)]
    cq = [
        fetch(w_qkv.at[:, pl.ds((t * PAIRS + p) * LANES, LANES)], wq.at[:, pl.ds((p * 3 + t) * LANES, LANES)])
        for p in range(PAIRS) for t in range(3)
    ]
    barrier = pltpu.get_barrier_semaphore()
    pl.semaphore_signal(barrier, inc=1, device_id={"frame": other}, device_id_type=MESH)
    cp = fetch(w_proj, wp)
    ce = fetch(w_expand, we)
    cr = fetch(w_reduce, wr)
    cc = [fetch(cot.at[0, place(s)], up0.at[s]) for s in range(N)]

    def vec(i):
        return vec_d[pl.ds(i, 1), :]

    attn_gain, attn_shift, query_bias, value_bias = vec(0), vec(1), vec(2), vec(3)
    proj_bias, mlp_gain, mlp_shift, reduce_bias = vec(4), vec(5), vec(6), vec(7)

    def limit(s):
        frame = s + z * (7 - 2 * s)
        return jnp.where(frame < cnt[0], res[0], 0)

    for ref in (n, sec, up, a, ge, gb):
        for s in range(N):
            ref[pl.ds(s * F + T, F - T), :] = jnp.zeros((F - T, ref.shape[1]), ref.dtype)
    for p in range(PAIRS):
        for s in range(N):
            gbl[p, pl.ds(s * F + T, F - T), :] = jnp.zeros((F - T, LANES), bf16)
    row = lax.broadcasted_iota(jnp.int32, (F, LANES), 0)
    lane = lax.broadcasted_iota(jnp.int32, (F, LANES), 1)
    low = lane < 64

    pl.semaphore_wait(barrier, 1)
    halo = pltpu.make_async_remote_copy(
        src_ref=tokens.at[0, place(N - 1)], dst_ref=x.at[N], send_sem=hsem.at[0], recv_sem=hsem.at[1],
        device_id={"frame": other}, device_id_type=MESH,
    )
    halo.start()

    def put_kv(s, p, keys, values):
        k[p, rows_of(s), :] = jnp.where(row < limit(s), keys, 0.0).astype(bf16)
        v[p, rows_of(s), pl.ds(0, LANES)] = jnp.where(
            row < T, values + value_bias[:, p * LANES:(p + 1) * LANES], 0.0
        ).astype(bf16)
        v[p, rows_of(s), pl.ds(LANES, LANES)] = jnp.ones((F, LANES), bf16)

    for c in cx + cq:
        c.wait()

    def project(s, carry):
        scaled, _ = normalise(x[s].astype(f32))
        n[live_rows_of(s), :] = (scaled * attn_gain + attn_shift).astype(bf16)
        joined = dot(n[rows_of(s), :], wq[...])
        for p in range(PAIRS):
            block = joined[:, p * D:(p + 1) * D]
            biased = (block[:, :LANES] + query_bias[:, p * LANES:(p + 1) * LANES]).astype(bf16)
            q[p, rows_of(s), :] = biased * jnp.asarray(0.125, bf16)
            put_kv(s, p, block[:, LANES:2 * LANES], block[:, 2 * LANES:])
        return carry

    lax.fori_loop(0, N, project, 0)

    halo.wait()
    scaled, _ = normalise(x[N].astype(f32))
    n[pl.ds(N * F, T), :] = (scaled * attn_gain + attn_shift).astype(bf16)
    n[pl.ds(N * F + T, F - T), :] = jnp.zeros((F - T, D), bf16)
    for p in range(PAIRS):
        block = dot(n[pl.ds(N * F, F), :], wq[:, pl.ds(p * D + LANES, 2 * LANES)])
        put_kv(N, p, block[:, :LANES], block[:, LANES:])

    def window(j):
        return list(range(max(j - 1, 0), j + 2))

    def span(j):
        w = window(j)
        return pl.ds(w[0] * F, len(w) * F)

    def bias_of(j):
        w = window(j)
        at = lax.broadcasted_iota(jnp.int32, (1, len(w) * F), 1)
        out = jnp.zeros((1, len(w) * F), f32)
        for i, s in enumerate(w):
            inside = (at >= i * F) & (at < (i + 1) * F)
            out = jnp.where(inside & (at >= i * F + limit(s)), NEG, out)
            out = jnp.where(inside & (at >= i * F + T), PAD, out)
        return out

    def half(value, h):
        zero = jnp.zeros_like(value)
        return jnp.where(low, value, zero) if h == 0 else jnp.where(low, zero, value)

    def weights_at(p, j, h):
        if j == 0:
            return e0.at[p, pl.ds(h * F, F)]
        return e.at[p * 3 + j - 1, pl.ds(h * F, F)]

    def forward(p, carry):
        order = [(j, h) for j in range(N) for h in range(2)]

        def scores(j, h):
            return dot(half(q[p, pl.ds(j * F, F), :], h), k[p, span(j), :], NT) + bias_of(j)

        s = scores(*order[0])
        held = []
        for i, (j, h) in enumerate(order):
            later = scores(*order[i + 1]) if i + 1 < len(order) else None
            largest = jnp.max(s, axis=1, keepdims=True)
            ex = jnp.exp(s - largest).astype(bf16)
            weights_at(p, j, h)[...] = ex
            o = dot(ex, v[p, span(j), :])
            total = o[:, LANES:]
            if j == 0:
                total = total + T * jnp.exp(NEG - largest)
            held.append((o[:, :LANES], 1.0 / total))
            if h == 1:
                (oa, ia), (ob, ib) = held
                held = []
                both = jnp.where(low, ia, ib)
                inv[p, pl.ds(j * F, F), :] = both
                bl[p, pl.ds(j * F, F), :] = (jnp.where(low, oa, ob) * both).astype(bf16)
            s = later
        return carry

    lax.fori_loop(0, PAIRS, forward, 0)

    for c in [cp, ce, cr] + cc:
        c.wait()
    acc_d[...] = jnp.zeros_like(acc_d)
    acc_ff[...] = jnp.zeros_like(acc_ff)
    live_row = lax.broadcasted_iota(jnp.int32, (T, D), 0)

    def mlp(j, carry):
        blended = jnp.concatenate([bl[p, live_rows_of(j), :] for p in range(PAIRS)], axis=1)
        hidden = x[j].astype(f32) + dot(blended, wp[...]) + proj_bias
        scaled, inverse = normalise(hidden)
        second = (scaled * mlp_gain + mlp_shift).astype(bf16)
        sec[live_rows_of(j), :] = second
        upstream = jnp.where(live_row < limit(j), up0[j].astype(f32), 0.0)
        up_low = upstream.astype(bf16)
        up[live_rows_of(j), :] = up_low
        output = hidden + reduce_bias
        grad_second = jnp.zeros((T, D), f32)
        for c in range(FF // CHUNK):
            cols = pl.ds(c * CHUNK, CHUNK)
            expanded = dot(second, we[:, cols]) + vec_ff[:, cols]
            gelu, slope = gelu_parts(expanded)
            low_gelu = gelu.astype(bf16)
            a[live_rows_of(j), cols] = low_gelu
            output = output + dot(low_gelu, wr[cols, :])
            grad = dot(up_low, wr[cols, :], NT) * slope
            grad_low = grad.astype(bf16)
            ge[live_rows_of(j), cols] = grad_low
            acc_ff[:, cols] += column_sum(grad_low.astype(f32))
            grad_second = grad_second + dot(grad_low, we[:, cols], NT)
        ostage[j] = output.astype(bf16)
        pltpu.make_async_copy(ostage.at[j], act_out.at[0, place(j)], osem.at[j]).start()
        acc_d[pl.ds(0, 1), :] += column_sum(upstream)
        acc_d[pl.ds(1, 1), :] += column_sum(grad_second * scaled)
        acc_d[pl.ds(2, 1), :] += column_sum(grad_second)
        grad_hidden = upstream + norm_back(grad_second, scaled, inverse, mlp_gain)
        gh[j] = grad_hidden
        branch = grad_hidden.astype(bf16)
        gb[live_rows_of(j), :] = branch
        acc_d[pl.ds(3, 1), :] += column_sum(branch.astype(f32))
        grad_blended = dot(branch, wp[...], NT).astype(bf16)
        for p in range(PAIRS):
            gbl[p, live_rows_of(j), :] = grad_blended[:, p * LANES:(p + 1) * LANES]
        return carry

    lax.fori_loop(0, N, mlp, 0)

    def pack(ref, base, block):
        block = block.astype(bf16)
        for t in range(block.shape[1] // LANES):
            ref[pl.ds(base + t * D, D), :] = block[:, t * LANES:(t + 1) * LANES]

    def pack_vectors(ref, base, rows, vectors):
        pieces = [w[:, t * LANES:(t + 1) * LANES] for w in vectors for t in range(w.shape[1] // LANES)]
        pieces.append(jnp.zeros((rows - len(pieces), LANES), f32))
        ref[pl.ds(base, rows), :] = jnp.concatenate(pieces, axis=0).astype(bf16)

    def big_weights(c, carry):
        cols = pl.ds(pl.multiple_of(c * D, LANES), D)
        base = pl.multiple_of(c * 3 * D, 16)
        pack(early, base, dot(sec[...], ge[:, cols], TN))
        pack(early, base + 12 * D, dot(up[...], a[:, cols], TN))
        return carry

    lax.fori_loop(0, FF // D, big_weights, 0)
    blended = jnp.concatenate([bl[p] for p in range(PAIRS)], axis=1)
    pack(early, 24 * D, dot(blended, gb[...], TN))
    pack_vectors(
        early, 27 * D, EARLY - 27 * D,
        [acc_d[pl.ds(0, 1), :], acc_ff[...], acc_d[pl.ds(1, 1), :], acc_d[pl.ds(2, 1), :], acc_d[pl.ds(3, 1), :]],
    )
    ce_out = pltpu.make_async_copy(early, early_out, osem.at[8])
    ce_out.start()

    def backward(p, carry):
        order = [(j, h) for j in (3, 2, 1, 0) for h in range(2)]
        prepared = {}

        def prepare(j):
            at = pl.ds(j * F, F)
            g = (gbl[p, at, :].astype(f32) * inv[p, at, :]).astype(bf16)
            product = g.astype(f32) * (-bl[p, at, :].astype(f32))
            high = product.astype(bf16)
            rest = pltpu.roll(product - high.astype(f32), 64, 1).astype(bf16)
            return g, high, rest

        def grad_weights(j, h):
            if j not in prepared:
                prepared[j] = prepare(j)
            g, high, rest = prepared[j]
            extra = jnp.where(low, high, rest) if h == 0 else jnp.where(low, rest, high)
            return dot(jnp.concatenate([half(g, h), extra], axis=1), v[p, span(j), :], NT)

        sums = {}

        def add(s, part):
            sums[s] = part if s not in sums else [y + w for y, w in zip(sums[s], part)]

        dp = grad_weights(*order[0])
        scores = []
        queries = []
        sent = None
        for i, (j, h) in enumerate(order):
            later = grad_weights(*order[i + 1]) if i + 1 < len(order) else None
            ds = (dp * weights_at(p, j, h)[...].astype(f32)).astype(bf16)
            scores.append(ds)
            queries.append(dot(ds, k[p, span(j), :]))
            if h == 1:
                at = pl.ds(j * F, F)
                gj[p, at, pl.ds(0, LANES)] = (jnp.where(low, queries[0], queries[1]) * 0.125).astype(bf16)
                qq = q[p, at, :]
                g = prepared[j][0]
                dk = dot(
                    jnp.concatenate([half(qq, 0), half(qq, 1)], axis=0), jnp.concatenate(scores, axis=0), TN
                ).T
                both = e0[p] if j == 0 else e[p * 3 + j - 1]
                dv = dot(jnp.concatenate([half(g, 0), half(g, 1)], axis=0), both, TN).T
                for t, s in enumerate(window(j)):
                    add(s, [dk[t * F:(t + 1) * F], dv[t * F:(t + 1) * F]])
                scores, queries = [], []
                if j == 3:
                    hsend[p, 0] = sums[N][0].astype(bf16)
                    hsend[p, 1] = sums[N][1].astype(bf16)
                    sent = pltpu.make_async_remote_copy(
                        src_ref=hsend.at[p], dst_ref=hrecv.at[p], send_sem=hsem.at[2 + p], recv_sem=hsem.at[5 + p],
                        device_id={"frame": other}, device_id_type=MESH,
                    )
                    sent.start()
            dp = later
        for s in range(N - 1):
            for t in range(2):
                gj[p, pl.ds(s * F, F), pl.ds((1 + t) * LANES, LANES)] = sums[s][t].astype(bf16)
        sent.wait()
        for t in range(2):
            gj[p, pl.ds(3 * F, F), pl.ds((1 + t) * LANES, LANES)] = (
                sums[3][t] + hrecv[p, t].astype(f32)
            ).astype(bf16)
        pack(late, pl.multiple_of(p * 3 * D, 16), dot(n[pl.ds(0, N * F), :], gj[p], TN))
        return carry

    lax.fori_loop(0, PAIRS, backward, 0)

    acc_d[...] = jnp.zeros_like(acc_d)

    def finish(j, carry):
        grads = jnp.concatenate([gj[p, rows_of(j), :] for p in range(PAIRS)], axis=1)
        for p in range(PAIRS):
            acc_d[pl.ds(2, 1), p * LANES:(p + 1) * LANES] += column_sum(grads[:, p * D:p * D + LANES].astype(f32))
            acc_d[pl.ds(3, 1), p * LANES:(p + 1) * LANES] += column_sum(
                grads[:, p * D + 2 * LANES:(p + 1) * D].astype(f32)
            )
        grad_normed = dot(grads, wq[...], NT)[:T]
        scaled, inverse = normalise(x[j].astype(f32))
        acc_d[pl.ds(0, 1), :] += column_sum(grad_normed * scaled)
        acc_d[pl.ds(1, 1), :] += column_sum(grad_normed)
        gstage[j] = gh[j] + norm_back(grad_normed, scaled, inverse, attn_gain)
        pltpu.make_async_copy(gstage.at[j], grad_out.at[0, place(j)], osem.at[4 + j]).start()
        return carry

    lax.fori_loop(0, N, finish, 0)
    pack_vectors(
        late, 9 * D, LATE - 9 * D,
        [acc_d[pl.ds(2, 1), :], acc_d[pl.ds(3, 1), :], acc_d[pl.ds(0, 1), :], acc_d[pl.ds(1, 1), :]],
    )
    cl_out = pltpu.make_async_copy(late, late_out, osem.at[9])
    cl_out.start()
    for j in range(N):
        pltpu.make_async_copy(ostage.at[j], act_out.at[0, place(j)], osem.at[j]).wait()
        pltpu.make_async_copy(gstage.at[j], grad_out.at[0, place(j)], osem.at[4 + j]).wait()
    ce_out.wait()
    cl_out.wait()


def run_main(tokens, cot, w_qkv, w_proj, w_expand, w_reduce, vec_d, vec_ff, res, cnt):
    hbm = pl.BlockSpec(memory_space=pl.ANY)
    vmem = pl.BlockSpec(memory_space=pltpu.VMEM)
    smem = pl.BlockSpec(memory_space=pltpu.SMEM)
    R = N * F
    V = pltpu.VMEM
    scratch = [
        V((N + 1, T, D), bf16), V((N, T, D), bf16), V((D, 3 * D), bf16), V((D, D), bf16), V((D, FF), bf16), V((FF, D), bf16),
        V((R + F, D), bf16), V((PAIRS, R, LANES), bf16), V((PAIRS, R + F, LANES), bf16), V((PAIRS, R + F, 2 * LANES), bf16),
        V((PAIRS, 2 * F, 2 * F), bf16), V((PAIRS * 3, 2 * F, 3 * F), bf16),
        V((PAIRS, R, LANES), bf16), V((PAIRS, R, LANES), f32), V((8, 128), f32),
        V((R, D), bf16), V((R, D), bf16), V((R, FF), bf16), V((R, FF), bf16), V((N, T, D), f32), V((R, D), bf16),
        V((PAIRS, R, LANES), bf16), V((PAIRS, R, D), bf16),
        V((PAIRS, 2, F, LANES), bf16), V((PAIRS, 2, F, LANES), bf16), V((N, T, D), bf16), V((N, T, D), f32),
        V((EARLY, LANES), bf16), V((LATE, LANES), bf16), V((8, D), f32), V((1, FF), f32),
        pltpu.SemaphoreType.DMA((24,)), pltpu.SemaphoreType.DMA((10,)), pltpu.SemaphoreType.DMA((8,)),
    ]
    return pl.pallas_call(
        main_kernel,
        out_shape=[
            jax.ShapeDtypeStruct((1, N, T, D), bf16), jax.ShapeDtypeStruct((1, N, T, D), f32),
            jax.ShapeDtypeStruct((EARLY, LANES), bf16), jax.ShapeDtypeStruct((LATE, LANES), bf16),
        ],
        in_specs=[hbm] * 6 + [vmem] * 2 + [smem] * 2,
        out_specs=[hbm] * 4,
        scratch_shapes=scratch,
        compiler_params=pltpu.CompilerParams(
            collective_id=0, has_side_effects=True, vmem_limit_bytes=63 * 2**20
        ),
    )(tokens, cot, w_qkv, w_proj, w_expand, w_reduce, vec_d, vec_ff, res, cnt)


def unpack(early, late):
    e = early.astype(f32)
    w = late.astype(f32)

    def block(rows, base):
        return jnp.concatenate([rows[base + t * D:base + (t + 1) * D] for t in range(3)], axis=1)

    g_we = jnp.concatenate([block(e, c * 3 * D) for c in range(4)], axis=1)
    g_wr = jnp.concatenate([block(e, (c + 4) * 3 * D).T for c in range(4)], axis=0)
    g_wp = block(e, 24 * D)
    tail = e[27 * D:27 * D + 24].reshape(-1)
    g_rb, g_eb, g_mg, g_ms, g_pb = tail[:384], tail[384:1920], tail[1920:2304], tail[2304:2688], tail[2688:3072]
    g_wq = jnp.concatenate(
        [w[(p * 3 + t) * D:(p * 3 + t + 1) * D] for t in range(3) for p in range(PAIRS)], axis=1
    )
    tail = w[9 * D:9 * D + 12].reshape(-1)
    g_qb, g_vb, g_ag, g_as = tail[:384], tail[384:768], tail[768:1152], tail[1152:1536]
    return (g_ag, g_as, g_wq, g_qb, g_vb, g_wp, g_pb, g_mg, g_ms, g_we, g_eb, g_wr, g_rb)


def body(
    tokens, attn_gain, attn_shift, w_qkv, query_bias, value_bias, w_proj, proj_bias, mlp_gain, mlp_shift,
    w_expand, expand_bias, w_reduce, reduce_bias, cotangent, resolution, frame_count,
):
    vec_d = jnp.stack(
        [y.astype(f32) for y in (attn_gain, attn_shift, query_bias, value_bias, proj_bias, mlp_gain, mlp_shift, reduce_bias)]
    )
    vec_ff = expand_bias.astype(f32).reshape(1, FF)
    act, grad, early, late = run_main(
        tokens, cotangent, w_qkv, w_proj, w_expand, w_reduce, vec_d, vec_ff, resolution, frame_count
    )
    early, late = lax.psum((early, late), ("clip", "frame"))
    grads = unpack(early, late)
    squares = sum(jnp.sum(g * g) for g in grads)
    return (act, grad) + grads + (jnp.sqrt(squares),)


def solution(mesh):
    data = P("clip", "frame", None, None)
    return jax.shard_map(
        body,
        mesh=mesh,
        in_specs=(data,) + (P(),) * 13 + (data, P("clip"), P("clip")),
        out_specs=(data, data) + (P(),) * 14,
        check_vma=False,
    )
```

time: 501 us -> 283 us (0.56); the launches traced: 495 us -> 283 us
  matrix products: 154 us -> 0 us
  waiting for transfers between devices: 71.2 us -> 152 us
  Pallas kernels: 0 us -> 75.3 us
  blocking collectives: 67.4 us -> 0 us
  other arithmetic: 79.7 us -> 13.1 us
  local copies, waits for them, and re-layouts: 80.2 us -> 17.3 us
  starting transfers between devices: 16.2 us -> 0.04 us
    dot_general x18 -> x0, matrix products: 154 us -> none  [the longest x1 22.9 us: attend_back(): jnp.einsum('fqhd,fkhd->fhqk', grad_heads, value_heads, preferred_element_...]
    psum x1, waiting for transfers between devices: 63.8 us -> 152 us  [body(): early, late = lax.psum((early, late), ('clip', 'frame'))]
    pallas_call x0 -> x1, Pallas kernels: none -> 75.3 us  [run_main(): pl.pallas_call(main_kernel, out_shape=[jax.ShapeDtypeStruct((1, N, T, D),...]
    psum x1 -> x0, blocking collectives: 67.4 us -> none  [body(): lax.psum((grad_attn_gain, grad_attn_shift, grad_w_qkv, grad_query_bias, g...]
    reshape x12 -> x1, local copies, waits for them, and re-layouts: 35.1 us -> 0.6 us  [body(): vec_ff = expand_bias.astype(f32).reshape(1, FF)]
    convert_element_type x10 -> x2, other arithmetic: 29.2 us -> 2.16 us  [the longest x1 2.03 us: unpack(): e = early.astype(f32)]
    reduce_sum x21 -> x6, other arithmetic: 35 us -> 10.8 us  [body(): squares = sum((jnp.sum(g * g) for g in grads))]
    slice x7 -> x1, local copies, waits for them, and re-layouts: 17.5 us -> 0.29 us  [block(): rows[base + t * D:base + (t + 1) * D]]
  transfers between devices with their start and end apart: 5 -> 1, of which waited for: 3 -> 1; matrix products, arithmetic and copies ran while one was open for 11% -> 1% of each run, Pallas kernels for 0% -> 0%
where the time goes in v1:
time: 283 us
  waiting for transfers between devices  152 us (54%)
  Pallas kernels  75.3 us (27%)
  between operations  25.1 us (9%)
  local copies, waits for them, and re-layouts  17.3 us (6%)
  other arithmetic  13.1 us (5%)
    psum x1, waiting for transfers between devices, body(): early, late = lax.psum((early, late), ('clip', 'frame'))  152 us
    pallas_call x1, Pallas kernels, run_main(): pl.pallas_call(main_kernel, out_shape=[jax.ShapeDtypeStruct((1, N, T, D),...  75.3 us
    unnamed x60, local copies, waits for them, and re-layouts  14 us
    reduce_sum x6, other arithmetic, body(): squares = sum((jnp.sum(g * g) for g in grads))  10.8 us
  transfers between devices with their start and end apart: 1, of which 1 were waited for; matrix products, arithmetic and copies ran while one was open for 1% of the time, Pallas kernels for 0%

profile of v1, /device:TPU:1, one launch (start us, length us, event | category | flops | bytes accessed | tf_op | source)
XLA Modules:
  0.0 282.6 jit_solution(13109945784897447542)
XLA Ops:
  7.3 2.4 copy.33.tokens
  9.7 1.1 copy.34.cot
  10.9 0.6 reshape.55.vec_ff
  12.8 0.6 stack.51.vec_d
  13.5 75.3 %shard_map.288 = (bf16[1,4,324,384]{3,2,1,0:T(8,128)(2,1)}, f32[1,4,324,384]{3,2,1,0:T(8,128)}, bf16[10752,128]{1,0:T(8,128)(2,1)}, bf16[3840,128]{1,0:T(8,128)(2,1)}) custom-call(bf16[1,4,324,384]{3,2,1,0:T(8,128)(2,1)} %copy.33.tokens, bf16[1,4,324,384]{3,2,1,0:T(8,128)(2,1)} %copy.34.cot, bf16[384,1152]{1,0:T(8,128)(2,1)} %w_qkv.1, ...), custom_call_target="tpu_custom_call" | custom-call | tf_op jit(solution)/shard_map/pallas_call | solution.py:403
  88.8 1.2 copy-done.6
  90.0 1.3 copy.35
  91.3 1.8 copy.36
  93.1 151.7 %all-reduce.3.cloned.1.call-done = (bf16[3840,128]{1,0:T(8,128)(2,1)}, bf16[10752,128]{1,0:T(8,128)(2,1)}) async-done(((bf16[3840,128]{1,0:T(8,128)(2,1)}, bf16[10752,128]{1,0:T(8,128)(2,1)}), (bf16[3840,128]{1,0:T(8,128)(2,1)}, bf16[10752,128]{1,0:T(8,128)(2,1)})) %all-reduce.3.cloned.1.call-update) | async-done | bytes 3735568 | tf_op jit(solution)/shard_map/psum | solution.py:449
  244.8 2.0 convert_element_type.5
  246.9 0.1 convert_element_type.4
  247.1 1.3 multiply_reduce_fusion.5
  248.4 2.3 copy-done
  250.7 0.3 fusion
  251.0 1.2 multiply_reduce_fusion.4
  252.7 0.1 maximum_bitcast_fusion.2
  252.7 1.1 copy-done.3
  254.0 0.5 copy-done.4
  254.4 1.3 multiply_reduce_fusion
  255.7 1.9 copy.37
  257.7 1.8 slice_dynamic-update-slice_fusion
  259.5 2.6 multiply_reduce_fusion.2
  262.1 2.9 %multiply_reduce_fusion.1 = f32[]{:T(128)} fusion(f32[384,1536]{1,0:T(8,128)} %get-tuple-element.83), kind=kLoop, calls=%fused_computation.2 | loop fusion | flops 1179647 | bytes 2359300 | tf_op jit(solution)/shard_map/reduce_sum | solution.py:451
  268.1 1.5 multiply_reduce_fusion.3
  (62 shorter events, 0.6 us)
Async XLA Ops:
  7.2 2.5 copy-start.7
  7.2 3.6 %copy-start.10 = (f32[384]{0:T(512)S(1)}, f32[384]{0:T(512)}, u32[]{:S(2)}) copy-start(f32[384]{0:T(512)} %param.18) | copy-start | bytes 4612
  7.2 3.6 %copy-start.11 = (f32[384]{0:T(512)S(1)}, f32[384]{0:T(512)}, u32[]{:S(2)}) copy-start(f32[384]{0:T(512)} %param.19) | copy-start | bytes 4612
  7.2 3.6 %copy-start.14 = (bf16[384]{0:T(512)(128)(2,1)S(1)}, bf16[384]{0:T(512)(128)(2,1)}, u32[]{:S(2)}) copy-start(bf16[384]{0:T(512)(128)(2,1)} %param.21) | copy-start | bytes 2308
  7.2 3.6 %copy-start.15 = (bf16[384]{0:T(512)(128)(2,1)S(1)}, bf16[384]{0:T(512)(128)(2,1)}, u32[]{:S(2)}) copy-start(bf16[384]{0:T(512)(128)(2,1)} %param.22) | copy-start | bytes 2308
  7.2 3.6 %copy-start.16 = (bf16[384]{0:T(512)(128)(2,1)S(1)}, bf16[384]{0:T(512)(128)(2,1)}, u32[]{:S(2)}) copy-start(bf16[384]{0:T(512)(128)(2,1)} %param.24) | copy-start | bytes 2308
  7.2 3.6 %copy-start.12 = (f32[384]{0:T(512)S(1)}, f32[384]{0:T(512)}, u32[]{:S(2)}) copy-start(f32[384]{0:T(512)} %param.25) | copy-start | bytes 4612
  7.3 3.6 %copy-start.13 = (f32[384]{0:T(512)S(1)}, f32[384]{0:T(512)}, u32[]{:S(2)}) copy-start(f32[384]{0:T(512)} %param.26) | copy-start | bytes 4612
  7.3 3.6 %copy-start.17 = (bf16[384]{0:T(512)(128)(2,1)S(1)}, bf16[384]{0:T(512)(128)(2,1)}, u32[]{:S(2)}) copy-start(bf16[384]{0:T(512)(128)(2,1)} %param.30) | copy-start | bytes 2308
  7.3 3.6 %copy-start.9 = (bf16[1536]{0:T(1024)(128)(2,1)S(1)}, bf16[1536]{0:T(1024)(128)(2,1)}, u32[]{:S(2)}) copy-start(bf16[1536]{0:T(1024)(128)(2,1)} %param.28) | copy-start | bytes 9220
  7.3 237.5 %all-reduce.3.cloned.1.call-start = ((), (), s32[]{:S(2)}) async-start(), calls=%async_computation | async-start | bytes 7471104 | tf_op jit(solution)/shard_map/psum | solution.py:449
  88.8 1.2 copy-start.6
  88.8 2.5 copy-start.5
  244.8 2.1 copy-start.8
  246.9 5.6 %copy-start.1 = (f32[10752,128]{1,0:T(8,128)}, f32[10752,128]{1,0:T(8,128)S(1)}, u32[]{:S(2)}) copy-start(f32[10752,128]{1,0:T(8,128)S(1)} %convert_element_type.5) | copy-start | bytes 16515076
  246.9 3.8 %copy-start = (bf16[10752,128]{1,0:T(8,128)(2,1)S(1)}, bf16[10752,128]{1,0:T(8,128)(2,1)}, u32[]{:S(2)}) copy-start(bf16[10752,128]{1,0:T(8,128)(2,1)} %get-tuple-element.49) | copy-start | bytes 8257540
  247.0 5.6 %copy-start.2 = (f32[3840,128]{1,0:T(8,128)}, f32[3840,128]{1,0:T(8,128)S(1)}, u32[]{:S(2)}) copy-start(f32[3840,128]{1,0:T(8,128)S(1)} %convert_element_type.4) | copy-start | bytes 5898244
  252.5 1.4 copy-start.3
  252.6 1.8 copy-start.4
Sparse Core Ops, SparseCore 0:
  88.9 155.8 all-reduce.2

commit v2 on v1

v2 whole, which is shorter than its diff:
```python
import functools
import jax
import jax.numpy as jnp
from jax import lax
from jax.sharding import PartitionSpec as P
from jax.experimental import pallas as pl
from jax.experimental.pallas import tpu as pltpu

T = 324
F = 336
D = 384
FF = 1536
N = 4
PAIRS = 3
EPS = 1e-6
NEG = -1e9
PAD = -1e30
LANES = 128
CHUNK = 512
R = N * F
f32 = jnp.float32
bf16 = jnp.bfloat16
NT = (((1,), (1,)), ((), ()))
NN = (((1,), (0,)), ((), ()))
TN = (((0,), (0,)), ((), ()))
MESH = pl.DeviceIdType.MESH


def dot(a, b, dims=NN):
    return lax.dot_general(a, b, dims, preferred_element_type=f32)


def rows_of(slot):
    return pl.ds(pl.multiple_of(slot * F, 16), F)


def live_rows_of(slot):
    return pl.ds(pl.multiple_of(slot * F, 16), T)


def normalise(x):
    centre = x - jnp.mean(x, axis=1, keepdims=True)
    spread = jnp.mean(centre * centre, axis=1, keepdims=True)
    inverse = lax.rsqrt(spread + EPS)
    return centre * inverse, inverse


def norm_back(grad, scaled, inverse, gain):
    e = grad * gain
    return inverse * (
        e - jnp.mean(e, axis=1, keepdims=True) - scaled * jnp.mean(e * scaled, axis=1, keepdims=True)
    )


def gelu_parts(x):
    u = jnp.exp(-0.5 * (x * x))
    t = 1.0 / (1.0 + 0.23164188844 * jnp.abs(x))
    p = t * (0.127414796 + t * (-0.142248368 + t * (0.7107068705 + t * (-0.7265760135 + t * 0.5307027145))))
    h = p * u
    cdf = jnp.where(x >= 0, 1.0 - h, h)
    return x * cdf, cdf + x * (u * 0.3989422804014327)


def column_sum(x):
    return jnp.sum(x, axis=0, keepdims=True)


def coordinates():
    clip = lax.axis_index("clip")
    z_hi = lax.axis_index("frame")
    core = clip % 2
    x = (clip // 2) % 4
    z_lo = (clip // 8) % 2
    y = clip // 16
    return x, y, 2 * z_hi + z_lo, core


def device_at(x, y, z, core):
    return {"clip": ((y * 2 + z % 2) * 4 + x) * 2 + core, "frame": z // 2}


def along(axis, step):
    x, y, z, core = coordinates()
    if axis == 0:
        x = (x + step) % 4
    elif axis == 1:
        y = (y + step) % 4
    else:
        z = (z + step) % 4
    return device_at(x, y, z, core)


def across():
    x, y, z, core = coordinates()
    return device_at(x, y, z, 1 - core)


def enter():
    barrier = pltpu.get_barrier_semaphore()
    pl.semaphore_signal(barrier, inc=1, device_id=across(), device_id_type=MESH)
    for axis in range(3):
        for step in (1, 2, 3):
            pl.semaphore_signal(barrier, inc=1, device_id=along(axis, step), device_id_type=MESH)


def entered():
    pl.semaphore_wait(pltpu.get_barrier_semaphore(), 10)


def total_of(parts):
    out = parts[0].astype(f32)
    for part in parts[1:]:
        out = out + part.astype(f32)
    return out.astype(bf16)


class Sum:
    def __init__(self, rows, scatter, fin, src, rcore, r1, w1, r2, w2, r3, sems):
        self.rows, self.scatter = rows, scatter
        self.src, self.fin, self.rcore, self.r1, self.w1, self.r2, self.w2, self.r3, self.sems = (
            src, fin, rcore, r1, w1, r2, w2, r3, sems)
        self.core = coordinates()[3]
        self.half, self.part, self.chunk = rows // 2, rows // 6, rows // 24
        self.sub = rows // 96 if scatter else rows // 24
        self.open = []
        self.count = 0

    @staticmethod
    def scratch(rows, scatter):
        sub = rows // 96 if scatter else rows // 24
        return [
            pltpu.VMEM((rows, LANES), bf16), pltpu.VMEM((rows // 2, LANES), bf16),
            pltpu.VMEM((3, 3, rows // 24, LANES), bf16), pltpu.VMEM((3, rows // 24, LANES), bf16),
            pltpu.VMEM((3, 3, sub, LANES) if scatter else (3, 4, sub, LANES), bf16), pltpu.VMEM((3, sub, LANES), bf16),
            pltpu.VMEM((3, 4, sub, LANES), bf16),
            pltpu.SemaphoreType.DMA((2, 2 + 9 * (5 if scatter else 4))),
        ]

    def send(self, src, dst, device):
        copy = pltpu.make_async_remote_copy(
            src_ref=src, dst_ref=dst, send_sem=self.sems.at[0, self.count], recv_sem=self.sems.at[1, self.count],
            device_id=device, device_id_type=MESH,
        )
        self.count += 1
        copy.start()
        self.open.append(copy)

    def arrive(self):
        for copy in self.open:
            copy.wait()
        self.open = []

    def spot(self, part, level):
        position = coordinates()[(part + level) % 3]
        return position

    def at(self, base, rows):
        return pl.ds(pl.multiple_of(base, 16), rows)

    def home(self, part, level):
        base = self.core * self.half + part * self.part
        if level >= 1:
            base = base + self.spot(part, 0) * self.chunk
        if level >= 2 and self.scatter:
            base = base + self.spot(part, 1) * self.sub
        return base

    def step0(self):
        away = (1 - self.core) * self.half
        self.send(self.src.at[self.at(away, self.half)], self.rcore, across())

    def step1(self):
        self.arrive()
        mine = self.at(self.core * self.half, self.half)
        self.src[mine, :] = total_of([self.src[mine, :], self.rcore[...]])
        for part in range(3):
            for step in (1, 2, 3):
                target = self.home(part, 0) + (self.spot(part, 0) + step) % 4 * self.chunk
                self.send(self.src.at[self.at(target, self.chunk)], self.r1.at[part, step - 1], along(part, step))

    def step2(self):
        self.arrive()
        for part in range(3):
            own = self.src[self.at(self.home(part, 1), self.chunk), :]
            total = total_of([own] + [self.r1[part, i] for i in range(3)])
            self.w1[part] = total
            if not self.scatter:
                self.r2[part, self.spot(part, 1)] = total
        for part in range(3):
            for step in (1, 2, 3):
                if self.scatter:
                    target = (self.spot(part, 1) + step) % 4 * self.sub
                    self.send(self.w1.at[part, self.at(target, self.sub)], self.r2.at[part, step - 1], along((part + 1) % 3, step))
                else:
                    self.send(self.w1.at[part], self.r2.at[part, self.spot(part, 1)], along((part + 1) % 3, step))

    def step3(self):
        self.arrive()
        for part in range(3):
            if self.scatter:
                own = self.w1[part, self.at(self.spot(part, 1) * self.sub, self.sub), :]
                total = total_of([own] + [self.r2[part, i] for i in range(3)])
            else:
                total = total_of([self.r2[part, i] for i in range(4)])
            self.w2[part] = total
            self.r3[part, self.spot(part, 2)] = total
        for part in range(3):
            for step in (1, 2, 3):
                self.send(self.w2.at[part], self.r3.at[part, self.spot(part, 2)], along((part + 2) % 3, step))

    def step4(self):
        self.arrive()
        for part in range(3):
            here = self.at(self.home(part, 2), self.sub)
            self.fin[here, :] = total_of([self.r3[part, i] for i in range(4)])
        if self.scatter:
            self.spread(1, 2, self.sub)
        else:
            self.spread(0, 1, self.chunk)

    def step5(self):
        self.arrive()
        if self.scatter:
            self.spread(0, 1, self.chunk)
        else:
            self.last()

    def step6(self):
        self.arrive()
        if self.scatter:
            self.last()

    def step7(self):
        self.arrive()

    def spread(self, axis, level, rows):
        for part in range(3):
            here = self.fin.at[self.at(self.home(part, level), rows)]
            for step in (1, 2, 3):
                self.send(here, here, along((part + axis) % 3, step))

    def last(self):
        here = self.fin.at[self.at(self.core * self.half, self.half)]
        self.send(here, here, across())


EARLY = 10752
LATES = ((0, 1), (2,))
LATE = tuple(-(-(len(g) * 9 * LANES + 16) // 384) * 384 for g in LATES)


def main_kernel(
    tokens, cot, w_qkv, w_proj, w_expand, w_reduce,
    v_ag, v_as, v_qb, v_vb, v_pb, v_mg, v_ms, v_rb, v_eb, res, cnt,
    act_out, grad_out, early_out, late0_out, late1_out,
    x, up0, wq, wp, we, wr, n, q, k, v, e0, e, bl, sec, up, a, ge, gh, gb, gbl, hrecv,
    acc_d, acc_ff, lsem, osem, hsem, *rest,
):
    z = lax.axis_index("frame")
    gj = a
    jobs = [Sum(EARLY, True, ge, *rest[:8]), Sum(LATE[0], False, *rest[8:17]), Sum(LATE[1], False, *rest[17:26])]
    early = jobs[0].src
    outs = [early_out, late0_out, late1_out]
    other = 1 - z

    def place(s):
        return s + z * (3 - 2 * s)

    local = []

    def fetch(src, dst):
        c = pltpu.make_async_copy(src, dst, lsem.at[len(local)])
        c.start()
        local.append(c)
        return c

    cx = [fetch(tokens.at[0, place(s)], x.at[s]) for s in range(N)]
    cq = [
        fetch(w_qkv.at[:, pl.ds((t * PAIRS + p) * LANES, LANES)], wq.at[:, pl.ds((p * 3 + t) * LANES, LANES)])
        for p in range(PAIRS) for t in range(3)
    ]
    enter()
    cp = fetch(w_proj, wp)
    ce = fetch(w_expand, we)
    cr = fetch(w_reduce, wr)
    cc = [fetch(cot.at[0, place(s)], up0.at[s]) for s in range(N)]

    attn_gain, attn_shift, query_bias, value_bias, proj_bias, mlp_gain, mlp_shift, reduce_bias, expand_bias = [
        ref[...].astype(f32).reshape(1, ref.shape[0])
        for ref in (v_ag, v_as, v_qb, v_vb, v_pb, v_mg, v_ms, v_rb, v_eb)
    ]

    def limit(s):
        frame = s + z * (7 - 2 * s)
        return jnp.where(frame < cnt[0], res[0], 0)

    for ref in (n, sec, up, a, gb, *[q.at[p] for p in range(PAIRS)]):
        for s in range(N):
            ref[pl.ds(s * F + T, F - T), :] = jnp.zeros((F - T, ref.shape[1]), ref.dtype)
    for p in range(PAIRS):
        for s in range(N):
            gbl[p, pl.ds(s * F + T, F - T), :] = jnp.zeros((F - T, LANES), bf16)
        for s in range(N + 1):
            k[p, pl.ds(s * F + T, F - T), :] = jnp.zeros((F - T, LANES), bf16)
            v[p, pl.ds(s * F + T, F - T), :] = jnp.zeros((F - T, LANES), bf16)
    for t in range(FF // LANES * N):
        ge[pl.ds(t * F + T, F - T), :] = jnp.zeros((F - T, LANES), bf16)
    row = lax.broadcasted_iota(jnp.int32, (F, LANES), 0)
    lane = lax.broadcasted_iota(jnp.int32, (F, LANES), 1)
    low = lane < 64

    entered()
    halo = pltpu.make_async_remote_copy(
        src_ref=tokens.at[0, place(N - 1)], dst_ref=x.at[N], send_sem=hsem.at[0], recv_sem=hsem.at[1],
        device_id={"frame": other}, device_id_type=MESH,
    )
    halo.start()

    def put_kv(s, p, keys, values):
        k[p, live_rows_of(s), :] = jnp.where(row[:T] < limit(s), keys, 0.0).astype(bf16)
        v[p, live_rows_of(s), :] = (values + value_bias[:, p * LANES:(p + 1) * LANES]).astype(bf16)

    for c in cx + cq:
        c.wait()

    def project(s, carry):
        scaled, _ = normalise(x[s].astype(f32))
        n[live_rows_of(s), :] = scaled.astype(bf16)
        joined = dot((scaled * attn_gain + attn_shift).astype(bf16), wq[...])
        for p in range(PAIRS):
            block = joined[:, p * D:(p + 1) * D]
            biased = (block[:, :LANES] + query_bias[:, p * LANES:(p + 1) * LANES]).astype(bf16)
            q[p, live_rows_of(s), :] = biased * jnp.asarray(0.125, bf16)
            put_kv(s, p, block[:, LANES:2 * LANES], block[:, 2 * LANES:])
        return carry

    lax.fori_loop(0, N, project, 0)

    halo.wait()
    scaled, _ = normalise(x[N].astype(f32))
    normed = (scaled * attn_gain + attn_shift).astype(bf16)
    for p in range(PAIRS):
        block = dot(normed, wq[:, pl.ds(p * D + LANES, 2 * LANES)])
        put_kv(N, p, block[:, :LANES], block[:, LANES:])

    def window(j):
        return list(range(max(j - 1, 0), j + 2))

    def span(j):
        w = window(j)
        return pl.ds(w[0] * F, len(w) * F)

    def bias_of(j):
        w = window(j)
        at = lax.broadcasted_iota(jnp.int32, (1, len(w) * F), 1)
        out = jnp.zeros((1, len(w) * F), f32)
        for i, s in enumerate(w):
            inside = (at >= i * F) & (at < (i + 1) * F)
            out = jnp.where(inside & (at >= i * F + limit(s)), NEG, out)
            out = jnp.where(inside & (at >= i * F + T), PAD, out)
        return out

    def half(value, h):
        zero = jnp.zeros_like(value)
        return jnp.where(low, value, zero) if h == 0 else jnp.where(low, zero, value)

    def values_at(p, j):
        return jnp.concatenate([v[p, span(j), :], jnp.ones((len(window(j)) * F, LANES), bf16)], axis=1)

    def weights_at(p, j, h):
        if j == 0:
            return e0.at[p, pl.ds(h * F, F)]
        return e.at[p * 3 + j - 1, pl.ds(h * F, F)]

    def forward(p, carry):
        order = [(j, h) for j in range(N) for h in range(2)]

        def scores(j, h):
            return dot(half(q[p, pl.ds(j * F, F), :], h), k[p, span(j), :], NT) + bias_of(j)

        s = scores(*order[0])
        held = []
        for i, (j, h) in enumerate(order):
            later = scores(*order[i + 1]) if i + 1 < len(order) else None
            largest = jnp.max(s, axis=1, keepdims=True)
            ex = jnp.exp(s - largest).astype(bf16)
            weights_at(p, j, h)[...] = ex
            o = dot(ex, values_at(p, j))
            total = o[:, LANES:]
            if j == 0:
                total = total + T * jnp.exp(NEG - largest)
            held.append((o[:, :LANES], 1.0 / total))
            if h == 1:
                (oa, ia), (ob, ib) = held
                held = []
                both = jnp.where(low, ia, ib)
                gh[j, :, pl.ds(pl.multiple_of(p * LANES, LANES), LANES)] = both[:T]
                bl[p, pl.ds(j * F, F), :] = jnp.where(low, oa, ob) * both
            s = later
        return carry

    lax.fori_loop(0, PAIRS, forward, 0)

    for c in [cp, ce, cr] + cc:
        c.wait()
    acc_d[...] = jnp.zeros_like(acc_d)
    acc_ff[...] = jnp.zeros_like(acc_ff)
    live_row = lax.broadcasted_iota(jnp.int32, (T, D), 0)

    def mlp(j, carry):
        blended = jnp.concatenate([bl[p, live_rows_of(j), :].astype(bf16) for p in range(PAIRS)], axis=1)
        hidden = x[j].astype(f32) + dot(blended, wp[...]) + proj_bias
        scaled, inverse = normalise(hidden)
        second = (scaled * mlp_gain + mlp_shift).astype(bf16)
        sec[live_rows_of(j), :] = second
        upstream = jnp.where(live_row < limit(j), up0[j].astype(f32), 0.0)
        up_low = upstream.astype(bf16)
        up[live_rows_of(j), :] = up_low
        output = hidden + reduce_bias
        grad_second = jnp.zeros((T, D), f32)
        for c in range(FF // CHUNK):
            cols = pl.ds(c * CHUNK, CHUNK)
            expanded = dot(second, we[:, cols]) + expand_bias[:, c * CHUNK:(c + 1) * CHUNK]
            gelu, slope = gelu_parts(expanded)
            low_gelu = gelu.astype(bf16)
            a[live_rows_of(j), cols] = low_gelu
            output = output + dot(low_gelu, wr[cols, :])
            grad = dot(up_low, wr[cols, :], NT) * slope
            grad_low = grad.astype(bf16)
            for t in range(CHUNK // LANES):
                at = pl.multiple_of((c * (CHUNK // LANES) + t) * R + j * F, 16)
                ge[pl.ds(at, T), :] = grad_low[:, t * LANES:(t + 1) * LANES]
            acc_ff[:, cols] += column_sum(grad_low.astype(f32))
            grad_second = grad_second + dot(grad_low, we[:, cols], NT)
        up0[j] = output.astype(bf16)
        pltpu.make_async_copy(up0.at[j], act_out.at[0, place(j)], osem.at[j]).start()
        acc_d[pl.ds(0, 1), :] += column_sum(upstream)
        acc_d[pl.ds(1, 1), :] += column_sum(grad_second * scaled)
        acc_d[pl.ds(2, 1), :] += column_sum(grad_second)
        grad_hidden = upstream + norm_back(grad_second, scaled, inverse, mlp_gain)
        branch = grad_hidden.astype(bf16)
        gb[live_rows_of(j), :] = branch
        acc_d[pl.ds(3, 1), :] += column_sum(branch.astype(f32))
        grad_blended = (dot(branch, wp[...], NT).astype(bf16).astype(f32) * gh[j]).astype(bf16)
        gh[j] = grad_hidden
        for p in range(PAIRS):
            gbl[p, live_rows_of(j), :] = grad_blended[:, p * LANES:(p + 1) * LANES]
        return carry

    lax.fori_loop(0, N, mlp, 0)

    def pack(ref, base, block):
        block = block.astype(bf16)
        for t in range(block.shape[1] // LANES):
            ref[pl.ds(base + t * D, D), :] = block[:, t * LANES:(t + 1) * LANES]

    def pack_vectors(ref, base, rows, vectors):
        pieces = [w[:, t * LANES:(t + 1) * LANES] for w in vectors for t in range(w.shape[1] // LANES)]
        pieces.append(jnp.zeros((rows - len(pieces), LANES), f32))
        ref[pl.ds(base, rows), :] = jnp.concatenate(pieces, axis=0).astype(bf16)

    def big_weights(c, carry):
        cols = pl.ds(pl.multiple_of(c * D, LANES), D)
        base = pl.multiple_of(c * 3 * D, 16)
        pack(early, base, dot(sec[...], jnp.concatenate([ge[pl.ds(pl.multiple_of((c * 3 + t) * R, 16), R), :] for t in range(3)], axis=1), TN))
        pack(early, base + 12 * D, dot(up[...], a[:, cols], TN))
        return carry

    lax.fori_loop(0, FF // D, big_weights, 0)
    blended = jnp.concatenate([bl[p].astype(bf16) for p in range(PAIRS)], axis=1)
    pack(early, 24 * D, dot(blended, gb[...], TN))
    pack_vectors(
        early, 27 * D, EARLY - 27 * D,
        [acc_d[pl.ds(0, 1), :], acc_ff[...], acc_d[pl.ds(1, 1), :], acc_d[pl.ds(2, 1), :], acc_d[pl.ds(3, 1), :]],
    )
    jobs[0].step0()

    def site(p, j):
        E = jobs[0]
        steps = {(0, 1): E.step1, (2, 3): E.step2}
        if (p, j) in steps:
            steps[(p, j)]()

    def backward(p):
        order = [(j, h) for j in (3, 2, 1, 0) for h in range(2)]
        prepared = {}

        def prepare(j):
            at = pl.ds(j * F, F)
            g = gbl[p, at, :]
            product = g.astype(f32) * (-bl[p, at, :])
            high = product.astype(bf16)
            rest = pltpu.roll(product - high.astype(f32), 64, 1).astype(bf16)
            return g, high, rest

        def grad_weights(j, h):
            if j not in prepared:
                prepared[j] = prepare(j)
            g, high, rest = prepared[j]
            extra = jnp.where(low, high, rest) if h == 0 else jnp.where(low, rest, high)
            return dot(jnp.concatenate([half(g, h), extra], axis=1), values_at(p, j), NT)

        sums = {}

        def add(s, part):
            sums[s] = part if s not in sums else [y + w for y, w in zip(sums[s], part)]

        dp = grad_weights(*order[0])
        scores = []
        queries = []
        sent = None
        for i, (j, h) in enumerate(order):
            later = grad_weights(*order[i + 1]) if i + 1 < len(order) else None
            ds = (dp * weights_at(p, j, h)[...].astype(f32)).astype(bf16)
            scores.append(ds)
            queries.append(dot(ds, k[p, span(j), :]))
            if h == 1:
                at = pl.ds(j * F, F)
                gj[at, pl.ds(p * D, LANES)] = (jnp.where(low, queries[0], queries[1]) * 0.125).astype(bf16)
                qq = q[p, at, :]
                g = prepared[j][0]
                dk = dot(
                    jnp.concatenate([half(qq, 0), half(qq, 1)], axis=0), jnp.concatenate(scores, axis=0), TN
                ).T
                both = e0[p] if j == 0 else e[p * 3 + j - 1]
                dv = dot(jnp.concatenate([half(g, 0), half(g, 1)], axis=0), both, TN).T
                for t, s in enumerate(window(j)):
                    add(s, [dk[t * F:(t + 1) * F], dv[t * F:(t + 1) * F]])
                scores, queries = [], []
                if j == 3:
                    sec[pl.ds(0, F), pl.ds(p * LANES, LANES)] = sums[N][0].astype(bf16)
                    sec[pl.ds(F, F), pl.ds(p * LANES, LANES)] = sums[N][1].astype(bf16)
                    sent = pltpu.make_async_remote_copy(
                        src_ref=sec.at[pl.ds(0, 2 * F), pl.ds(p * LANES, LANES)], dst_ref=hrecv.at[p], send_sem=hsem.at[2 + p], recv_sem=hsem.at[5 + p],
                        device_id={"frame": other}, device_id_type=MESH,
                    )
                    sent.start()
            dp = later
            if h == 1:
                site(p, j)
        for s in range(N - 1):
            for t in range(2):
                gj[pl.ds(s * F, F), pl.ds(p * D + (1 + t) * LANES, LANES)] = sums[s][t].astype(bf16)
        sent.wait()
        for t in range(2):
            gj[pl.ds(3 * F, F), pl.ds(p * D + (1 + t) * LANES, LANES)] = (
                sums[3][t] + hrecv[p, pl.ds(t * F, F), :].astype(f32)
            ).astype(bf16)
        group = 0 if p in LATES[0] else 1
        at = LATES[group].index(p)
        columns = gj[:, pl.ds(p * D, D)]
        pack(jobs[1 + group].src, at * 3 * D, dot(n[...], columns, TN))
        columns_sum[p] = column_sum(columns.astype(f32))
        if at == len(LATES[group]) - 1:
            base = len(LATES[group]) * 3 * D
            pack_vectors(jobs[1 + group].src, base, LATE[group] - base, [columns_sum[i] for i in LATES[group]])
            jobs[1 + group].step0()

    columns_sum = {}
    for p in range(PAIRS):
        backward(p)

    def tail(finish):
        E, A, B = jobs
        E.step3(); A.step1()
        finish(0, 0)
        B.step1()
        finish(1, 0)
        E.step4(); A.step2()
        finish(2, 0)
        B.step2()
        finish(3, 0)
        A.step3()
        E.step5()
        B.step3()
        A.step4()
        B.step4()
        E.step6()
        A.step5()
        B.step5()
        A.step6(); B.step6(); E.step7()

    def finish(j, carry):
        grad_normed = dot(gj[live_rows_of(j), pl.ds(0, 3 * D)], wq[...], NT)
        scaled, inverse = normalise(x[j].astype(f32))
        gh[j] = gh[j] + norm_back(grad_normed, scaled, inverse, attn_gain)
        pltpu.make_async_copy(gh.at[j], grad_out.at[0, :, place(j), :], osem.at[4 + j]).start()
        return carry

    tail(finish)
    for i, job in enumerate(jobs):
        copy = pltpu.make_async_copy(job.fin.at[pl.ds(0, job.rows)], outs[i], osem.at[8 + i])
        copy.start()
    for j in range(N):
        pltpu.make_async_copy(up0.at[j], act_out.at[0, place(j)], osem.at[j]).wait()
        pltpu.make_async_copy(gh.at[j], grad_out.at[0, :, place(j), :], osem.at[4 + j]).wait()
    for i, job in enumerate(jobs):
        pltpu.make_async_copy(job.fin.at[pl.ds(0, job.rows)], outs[i], osem.at[8 + i]).wait()


def run_main(tokens, cot, w_qkv, w_proj, w_expand, w_reduce, *rest):
    hbm = pl.BlockSpec(memory_space=pl.ANY)
    vmem = pl.BlockSpec(memory_space=pltpu.VMEM)
    smem = pl.BlockSpec(memory_space=pltpu.SMEM)
    V = pltpu.VMEM
    scratch = [
        V((N + 1, T, D), bf16), V((N, T, D), bf16), V((D, 3 * D), bf16), V((D, D), bf16), V((D, FF), bf16), V((FF, D), bf16),
        V((R, D), bf16), V((PAIRS, R, LANES), bf16), V((PAIRS, R + F, LANES), bf16), V((PAIRS, R + F, LANES), bf16),
        V((PAIRS, 2 * F, 2 * F), bf16), V((PAIRS * 3, 2 * F, 3 * F), bf16),
        V((PAIRS, R, LANES), f32),
        V((R, D), bf16), V((R, D), bf16), V((R, FF), bf16), V((FF // LANES * R, LANES), bf16), V((N, T, D), f32), V((R, D), bf16),
        V((PAIRS, R, LANES), bf16),
        V((PAIRS, 2 * F, LANES), bf16), V((8, D), f32), V((1, FF), f32),
        pltpu.SemaphoreType.DMA((24,)), pltpu.SemaphoreType.DMA((11,)), pltpu.SemaphoreType.DMA((8,)),
    ] + Sum.scratch(EARLY, True) + [
        y for rows in LATE for y in [V((rows, LANES), bf16)] + Sum.scratch(rows, False)
    ]
    return pl.pallas_call(
        main_kernel,
        out_shape=[
            jax.ShapeDtypeStruct((1, N, T, D), bf16), jax.ShapeDtypeStruct((1, T, N, D), f32),
            jax.ShapeDtypeStruct((EARLY, LANES), bf16), jax.ShapeDtypeStruct((LATE[0], LANES), bf16),
            jax.ShapeDtypeStruct((LATE[1], LANES), bf16),
        ],
        in_specs=[hbm] * 6 + [vmem] * 9 + [smem] * 2,
        out_specs=[hbm] * 5,
        scratch_shapes=scratch,
        compiler_params=pltpu.CompilerParams(
            collective_id=0, has_side_effects=True, vmem_limit_bytes=66_900_000
        ),
    )(tokens, cot, w_qkv, w_proj, w_expand, w_reduce, *rest)


def final_kernel(
    early_in, late0_in, late1_in, wq_in, gain_ref, shift_ref,
    o_ag, o_as, o_wq, o_qb, o_vb, o_wp, o_pb, o_mg, o_ms, o_we, o_eb, o_wr, o_rb, o_norm,
    early, late0, late1, wq, s_wq, s_wp, s_we, s_wr, isem, osem,
):
    half = 12 * D
    pieces = [
        (early_in.at[pl.ds(half, half)], early.at[pl.ds(half, half)]), (early_in.at[pl.ds(0, half)], early.at[pl.ds(0, half)]),
        (early_in.at[pl.ds(2 * half, EARLY - 2 * half)], early.at[pl.ds(2 * half, EARLY - 2 * half)]),
        (late0_in, late0), (late1_in, late1), (wq_in, wq),
    ]
    fetches = [pltpu.make_async_copy(src, dst, isem.at[i]) for i, (src, dst) in enumerate(pieces)]
    for copy in fetches:
        copy.start()

    def square(total, block):
        return total + jnp.sum(block * block, axis=0, keepdims=True)

    total = jnp.zeros((1, LANES), f32)
    stores = []

    def store(src, dst):
        copy = pltpu.make_async_copy(src, dst, osem.at[len(stores)])
        copy.start()
        stores.append(copy)

    fetches[0].wait()
    for c in range(12):
        block = early[pl.ds(half + c * D, D), :].astype(f32)
        s_wr[pl.ds(c * LANES, LANES), :] = block.T
        total = square(total, block)
    store(s_wr, o_wr)
    fetches[1].wait()
    for c in range(12):
        block = early[pl.ds(c * D, D), :].astype(f32)
        s_we[:, pl.ds(c * LANES, LANES)] = block
        total = square(total, block)
    store(s_we, o_we)
    fetches[2].wait()
    for c in range(3):
        block = early[pl.ds(2 * half + c * D, D), :].astype(f32)
        s_wp[:, pl.ds(c * LANES, LANES)] = block
        total = square(total, block)
    store(s_wp, o_wp)
    tail = early[pl.ds(27 * D, 32), :].astype(f32)
    total = square(total, tail[:24])
    lines = [tail[i:i + 1] for i in range(24)]

    def line(parts):
        return jnp.concatenate(parts, axis=1).reshape(len(parts) * LANES)

    o_rb[...] = line(lines[:3])
    o_eb[...] = line(lines[3:15])
    o_mg[...] = line(lines[15:18])
    o_ms[...] = line(lines[18:21])
    o_pb[...] = line(lines[21:24])

    def column(ref):
        row = ref[...].reshape(1, D)
        return jnp.broadcast_to(row, (LANES, D)).T

    gain, shift = column(gain_ref), column(shift_ref)
    for copy in fetches[3:]:
        copy.wait()
    along_gain = jnp.zeros((D, LANES), f32)
    along_shift = jnp.zeros((D, LANES), f32)
    sums = {}
    for group, ref in ((0, late0), (1, late1)):
        pairs = LATES[group]
        extra = ref[pl.ds(len(pairs) * 3 * D, 16), :].astype(f32)
        for i, p in enumerate(pairs):
            for t in range(3):
                moment = ref[pl.ds((i * 3 + t) * D, D), :].astype(f32)
                summed = extra[i * 3 + t:i * 3 + t + 1]
                sums[t, p] = summed
                cols = pl.ds((t * PAIRS + p) * LANES, LANES)
                weight = wq[:, cols].astype(f32)
                block = gain * moment + shift * summed
                s_wq[:, cols] = block
                total = square(total, block)
                along_gain = along_gain + weight * moment
                along_shift = along_shift + weight * summed
    store(s_wq, o_wq)
    grad_gain = jnp.sum(along_gain.T, axis=0, keepdims=True)
    grad_shift = jnp.sum(along_shift.T, axis=0, keepdims=True)
    o_ag[...] = grad_gain.reshape(D)
    o_as[...] = grad_shift.reshape(D)
    o_qb[...] = line([sums[0, p] for p in range(PAIRS)])
    o_vb[...] = line([sums[2, p] for p in range(PAIRS)])
    for p in range(PAIRS):
        total = square(square(total, sums[0, p]), sums[2, p])
        cols = slice(p * LANES, (p + 1) * LANES)
        total = square(square(total, grad_gain[:, cols]), grad_shift[:, cols])
    o_norm[...] = jnp.sqrt(jnp.sum(total, axis=1, keepdims=True))
    for copy in stores:
        copy.wait()


def run_final(early, late0, late1, w_qkv, gain, shift):
    hbm = pl.BlockSpec(memory_space=pl.ANY)
    vmem = pl.BlockSpec(memory_space=pltpu.VMEM)
    V = pltpu.VMEM
    vector = jax.ShapeDtypeStruct((D,), f32)

    def matrix(a, b):
        return jax.ShapeDtypeStruct((a, b), f32)

    shapes = [
        vector, vector, matrix(D, 3 * D), vector, vector, matrix(D, D), vector, vector, vector, matrix(D, FF),
        jax.ShapeDtypeStruct((FF,), f32), matrix(FF, D), vector, matrix(1, 1),
    ]
    return pl.pallas_call(
        final_kernel,
        out_shape=shapes,
        in_specs=[hbm] * 4 + [vmem] * 2,
        out_specs=[hbm if len(s.shape) == 2 and s.shape[0] > 1 else vmem for s in shapes],
        scratch_shapes=[
            V((EARLY, LANES), bf16), V((LATE[0], LANES), bf16), V((LATE[1], LANES), bf16), V((D, 3 * D), bf16),
            V((D, 3 * D), f32), V((D, D), f32), V((D, FF), f32), V((FF, D), f32),
            pltpu.SemaphoreType.DMA((6,)), pltpu.SemaphoreType.DMA((4,)),
        ],
        compiler_params=pltpu.CompilerParams(vmem_limit_bytes=40 * 2**20),
    )(early, late0, late1, w_qkv, gain, shift)


def body(
    tokens, attn_gain, attn_shift, w_qkv, query_bias, value_bias, w_proj, proj_bias, mlp_gain, mlp_shift,
    w_expand, expand_bias, w_reduce, reduce_bias, cotangent, resolution, frame_count,
):
    act, grad, early, late0, late1 = run_main(
        tokens, cotangent, w_qkv, w_proj, w_expand, w_reduce, attn_gain, attn_shift, query_bias, value_bias,
        proj_bias, mlp_gain, mlp_shift, reduce_bias, expand_bias, resolution, frame_count,
    )
    *grads, norm = run_final(early, late0, late1, w_qkv, attn_gain, attn_shift)
    return (act, jnp.transpose(grad, (0, 2, 1, 3)), *grads, norm.reshape(()))


def solution(mesh):
    data = P("clip", "frame", None, None)
    return jax.shard_map(
        body,
        mesh=mesh,
        in_specs=(data,) + (P(),) * 13 + (data, P("clip"), P("clip")),
        out_specs=(data, data) + (P(),) * 14,
        check_vma=False,
    )
```

time: 283 us -> 123 us (0.43)
  waiting for transfers between devices: 152 us -> 0 us
  Pallas kernels: 75.3 us -> 111 us
  between operations: 25.1 us -> 2.13 us
  other arithmetic: 13.1 us -> 0 us
  local copies, waits for them, and re-layouts: 17.3 us -> 9.13 us
    psum x1 -> x0, waiting for transfers between devices: 152 us -> none  [body(): early, late = lax.psum((early, late), ('clip', 'frame'))]
    pallas_call x1, Pallas kernels: 75.3 us -> 106 us  [run_main(): pl.pallas_call(main_kernel, out_shape=[jax.ShapeDtypeStruct((1, N, T, D),...]
    reduce_sum x6 -> x0, other arithmetic: 10.8 us -> none  [body(): squares = sum((jnp.sum(g * g) for g in grads))]
    pallas_call x0 -> x1, Pallas kernels: none -> 5.53 us  [run_final(): pl.pallas_call(final_kernel, out_shape=shapes, in_specs=[hbm] * 4 + [vmem...]
    unnamed x60 -> x20, local copies, waits for them, and re-layouts: 14 us -> 9.13 us
  transfers between devices with their start and end apart: 1 -> 0, of which waited for: 1 -> 0; matrix products, arithmetic and copies ran while one was open for 1% -> 0% of each run, Pallas kernels for 0% -> 0%
where the time goes in v2:
time: 123 us
  Pallas kernels  111 us (90%)
  local copies, waits for them, and re-layouts  9.13 us (7%)
  between operations  2.13 us (2%)
    pallas_call x1, Pallas kernels, run_main(): pl.pallas_call(main_kernel, out_shape=[jax.ShapeDtypeStruct((1, N, T, D),...  106 us
    unnamed x20, local copies, waits for them, and re-layouts  9.13 us
    pallas_call x1, Pallas kernels, run_final(): pl.pallas_call(final_kernel, out_shape=shapes, in_specs=[hbm] * 4 + [vmem...  5.53 us

profile of v2, /device:TPU:1, one launch (start us, length us, event | category | flops | bytes accessed | tf_op | source)
XLA Modules:
  0.0 122.6 jit_solution(10987208856032399538)
XLA Ops:
  0.6 0.0 copy-start.7
  2.0 2.3 %copy.33.tokens = bf16[1,4,324,384]{3,2,1,0:T(8,128)(2,1)} copy(bf16[1,4,324,384]{3,1,2,0:T(4,128)(2,1)} %param.17) | data formatting | bytes 1990656 | tf_op args[0]
  4.3 0.0 copy-done.7
  4.3 1.1 copy.34.cot
  5.4 105.8 %shard_map.288 = (bf16[1,4,324,384]{3,2,1,0:T(8,128)(2,1)}, f32[1,324,4,384]{3,2,1,0:T(4,128)}, bf16[10752,128]{1,0:T(8,128)(2,1)}, bf16[2688,128]{1,0:T(8,128)(2,1)}, bf16[1536,128]{1,0:T(8,128)(2,1)}) custom-call(bf16[1,4,324,384]{3,2,1,0:T(8,128)(2,1)} %copy.33.tokens, bf16[1,4,324,384]{3,2,1,0:T(8,128)(2,1)} %copy.34.cot, bf16[384,1152]{1,0:T(8,128)(2,1)} %wq_in.1, ...), custom_call_target="tpu_custom_call" | custom-call | tf_op jit(solution)/shard_map/pallas_call | solution.py:618
  111.2 0.0 copy-start
  111.2 0.0 copy-start.2
  111.2 0.0 copy-start.3
  111.2 0.0 copy-start.4
  111.3 0.0 copy-start.5
  111.3 2.7 %copy.35 = bf16[1,4,324,384]{3,1,2,0:T(4,128)(2,1)} copy(bf16[1,4,324,384]{3,2,1,0:T(8,128)(2,1)} %get-tuple-element.54) | data formatting | bytes 1990656
  113.9 0.0 copy-done
  113.9 0.0 copy-done.2
  113.9 0.0 copy-done.3
  114.0 0.0 copy-done.4
  114.0 0.0 copy-done.5
  114.0 0.0 copy-start.1
  114.0 1.8 %copy-done.1 = bf16[10752,128]{1,0:T(8,128)(2,1)S(1)} copy-done((bf16[10752,128]{1,0:T(8,128)(2,1)S(1)}, bf16[10752,128]{1,0:T(8,128)(2,1)}, u32[]{:S(2)}) %copy-start.1) | copy-done | bytes 2752536
  115.7 0.0 copy-start.6
  115.8 5.5 %shard_map.289 = (f32[384]{0:T(512)}, f32[384]{0:T(512)}, f32[384,1152]{1,0:T(8,128)}, f32[384]{0:T(512)}, f32[384]{0:T(512)}, /*index=5*/f32[384,384]{1,0:T(8,1...) custom-call(bf16[10752,128]{1,0:T(8,128)(2,1)S(1)} %copy-done.1, ...), custom_call_target="tpu_custom_call" | custom-call | tf_op jit(solution)/shard_map/pallas_call | solution.py:745
  121.3 0.0 copy-done.6
  121.3 1.3 %copy.39 = f32[1,4,324,384]{3,1,2,0:T(4,128)} copy(f32[1,4,324,384]{3,1,2,0:T(4,128)S(1)} %bitcast.2) | data formatting | bytes 3981312
Async XLA Ops:
  0.6 3.7 %copy-start.7 = (bf16[1,4,324,384]{3,1,2,0:T(4,128)(2,1)S(1)}, bf16[1,4,324,384]{3,1,2,0:T(4,128)(2,1)}, u32[]{:S(2)}) copy-start(bf16[1,4,324,384]{3,1,2,0:T(4,128)(2,1)} %param.31) | copy-start | bytes 2985988
  111.2 2.7 %copy-start = (bf16[384,1152]{1,0:T(8,128)(2,1)S(1)}, bf16[384,1152]{1,0:T(8,128)(2,1)}, u32[]{:S(2)}) copy-start(bf16[384,1152]{1,0:T(8,128)(2,1)} %wq_in.1) | copy-start | bytes 2654212
  111.2 2.7 %copy-start.2 = (bf16[2688,128]{1,0:T(8,128)(2,1)S(1)}, bf16[2688,128]{1,0:T(8,128)(2,1)}, u32[]{:S(2)}) copy-start(bf16[2688,128]{1,0:T(8,128)(2,1)} %get-tuple-element.38.late0_in) | copy-start | bytes 2064388
  111.2 2.7 %copy-start.3 = (bf16[1536,128]{1,0:T(8,128)(2,1)S(1)}, bf16[1536,128]{1,0:T(8,128)(2,1)}, u32[]{:S(2)}) copy-start(bf16[1536,128]{1,0:T(8,128)(2,1)} %get-tuple-element.39.late1_in) | copy-start | bytes 1179652
  111.2 2.7 %copy-start.4 = (f32[384]{0:T(512)S(1)}, f32[384]{0:T(512)}, u32[]{:S(2)}) copy-start(f32[384]{0:T(512)} %gain_ref.1) | copy-start | bytes 4612
  111.3 2.7 %copy-start.5 = (f32[384]{0:T(512)S(1)}, f32[384]{0:T(512)}, u32[]{:S(2)}) copy-start(f32[384]{0:T(512)} %shift_ref.1) | copy-start | bytes 4612
  114.0 1.8 %copy-start.1 = (bf16[10752,128]{1,0:T(8,128)(2,1)S(1)}, bf16[10752,128]{1,0:T(8,128)(2,1)}, u32[]{:S(2)}) copy-start(bf16[10752,128]{1,0:T(8,128)(2,1)} %get-tuple-element.37.early_in) | copy-start | bytes 8257540
  115.7 5.5 %copy-start.6 = (f32[1,324,4,384]{3,2,1,0:T(4,128)S(1)}, f32[1,324,4,384]{3,2,1,0:T(4,128)}, u32[]{:S(2)}) copy-start(f32[1,324,4,384]{3,2,1,0:T(4,128)} %get-tuple-element.36) | copy-start | bytes 5971972

commit v3 on v2

v3 whole, which is shorter than its diff:
```python
import functools
import jax
import jax.numpy as jnp
from jax import lax
from jax.sharding import PartitionSpec as P
from jax.experimental import pallas as pl
from jax.experimental.pallas import tpu as pltpu

T = 324
F = 336
D = 384
FF = 1536
N = 4
PAIRS = 3
EPS = 1e-6
NEG = -1e9
PAD = -1e30
LANES = 128
CHUNK = 256
MLP_FRAMES = 2
R = N * F
f32 = jnp.float32
bf16 = jnp.bfloat16
NT = (((1,), (1,)), ((), ()))
NN = (((1,), (0,)), ((), ()))
TN = (((0,), (0,)), ((), ()))
MESH = pl.DeviceIdType.MESH


def dot(a, b, dims=NN):
    return lax.dot_general(a, b, dims, preferred_element_type=f32)


def rows_of(slot):
    return pl.ds(pl.multiple_of(slot * F, 16), F)


def live_rows_of(slot):
    return pl.ds(pl.multiple_of(slot * F, 16), T)


def normalise(x):
    centre = x - jnp.mean(x, axis=1, keepdims=True)
    spread = jnp.mean(centre * centre, axis=1, keepdims=True)
    inverse = lax.rsqrt(spread + EPS)
    return centre * inverse, inverse


def norm_back(grad, scaled, inverse, gain):
    e = grad * gain
    return inverse * (
        e - jnp.mean(e, axis=1, keepdims=True) - scaled * jnp.mean(e * scaled, axis=1, keepdims=True)
    )


def gelu_parts(x):
    u = jnp.exp(-0.5 * (x * x))
    t = 1.0 / (1.0 + 0.23164188844 * jnp.abs(x))
    p = t * (0.127414796 + t * (-0.142248368 + t * (0.7107068705 + t * (-0.7265760135 + t * 0.5307027145))))
    h = p * u
    cdf = jnp.where(x >= 0, 1.0 - h, h)
    return x * cdf, cdf + x * (u * 0.3989422804014327)


def column_sum(x):
    return jnp.sum(x, axis=0, keepdims=True)


def coordinates():
    clip = lax.axis_index("clip")
    z_hi = lax.axis_index("frame")
    core = clip % 2
    x = (clip // 2) % 4
    z_lo = (clip // 8) % 2
    y = clip // 16
    return x, y, 2 * z_hi + z_lo, core


def device_at(x, y, z, core):
    return {"clip": ((y * 2 + z % 2) * 4 + x) * 2 + core, "frame": z // 2}


def along(axis, step):
    x, y, z, core = coordinates()
    if axis == 0:
        x = (x + step) % 4
    elif axis == 1:
        y = (y + step) % 4
    else:
        z = (z + step) % 4
    return device_at(x, y, z, core)


def across():
    x, y, z, core = coordinates()
    return device_at(x, y, z, 1 - core)


def enter():
    barrier = pltpu.get_barrier_semaphore()
    pl.semaphore_signal(barrier, inc=1, device_id=across(), device_id_type=MESH)
    for axis in range(3):
        for step in (1, 2, 3):
            pl.semaphore_signal(barrier, inc=1, device_id=along(axis, step), device_id_type=MESH)


def entered():
    pl.semaphore_wait(pltpu.get_barrier_semaphore(), 10)


def total_of(parts):
    out = parts[0].astype(f32)
    for part in parts[1:]:
        out = out + part.astype(f32)
    return out.astype(bf16)


def strip(base, rows):
    return pl.ds(pl.multiple_of(base, 16), rows)


class Sum:
    def __init__(self, rows, scatter, fin, offset, src, rcore, r1, w1, r2, w2, r3, sems):
        self.rows, self.scatter, self.offset = rows, scatter, offset
        self.src, self.fin, self.rcore, self.r1, self.w1, self.r2, self.w2, self.r3, self.sems = (
            src, fin, rcore, r1, w1, r2, w2, r3, sems)
        self.half, self.part, self.chunk = rows // 2, rows // 6, rows // 24
        self.sub = rows // 96 if scatter else rows // 24

    @staticmethod
    def scratch(rows, scatter):
        sub = rows // 96 if scatter else rows // 24
        return [
            pltpu.VMEM((rows, LANES), bf16), pltpu.VMEM((rows // 2, LANES), bf16),
            pltpu.VMEM((3, 3, rows // 24, LANES), bf16), pltpu.VMEM((3, rows // 24, LANES), bf16),
            pltpu.VMEM((3, 3, sub, LANES) if scatter else (3, 4, sub, LANES), bf16), pltpu.VMEM((3, sub, LANES), bf16),
            pltpu.VMEM((3, 4, sub, LANES), bf16),
            pltpu.SemaphoreType.DMA((2, 2 + 9 * (5 if scatter else 4))),
        ]

    def spot(self, part, level):
        return coordinates()[(part + level) % 3]

    def home(self, part, level):
        base = coordinates()[3] * self.half + part * self.part
        if level >= 1:
            base = base + self.spot(part, 0) * self.chunk
        if level >= 2 and self.scatter:
            base = base + self.spot(part, 1) * self.sub
        return base

    def copies(self, stage):
        core = coordinates()[3]
        out = []
        last = 6 if self.scatter else 5
        if stage == 0:
            out.append((self.src.at[strip((1 - core) * self.half, self.half)], self.rcore, across()))
        elif stage == last:
            here = self.fin.at[strip(self.offset + core * self.half, self.half)]
            out.append((here, here, across()))
        else:
            for part in range(3):
                for step in (1, 2, 3):
                    if stage == 1:
                        target = self.home(part, 0) + (self.spot(part, 0) + step) % 4 * self.chunk
                        out.append((self.src.at[strip(target, self.chunk)], self.r1.at[part, step - 1], along(part, step)))
                    elif stage == 2 and self.scatter:
                        target = (self.spot(part, 1) + step) % 4 * self.sub
                        out.append((self.w1.at[part, strip(target, self.sub)], self.r2.at[part, step - 1], along((part + 1) % 3, step)))
                    elif stage == 2:
                        out.append((self.w1.at[part], self.r2.at[part, self.spot(part, 1)], along((part + 1) % 3, step)))
                    elif stage == 3:
                        out.append((self.w2.at[part], self.r3.at[part, self.spot(part, 2)], along((part + 2) % 3, step)))
                    else:
                        axis, level, rows = (1, 2, self.sub) if self.scatter and stage == 4 else (0, 1, self.chunk)
                        here = self.fin.at[strip(self.offset + self.home(part, level), rows)]
                        out.append((here, here, along((part + axis) % 3, step)))
        first = 0 if stage == 0 else 1 + 9 * (stage - 1)
        return [
            pltpu.make_async_remote_copy(
                src_ref=src, dst_ref=dst, send_sem=self.sems.at[0, first + i], recv_sem=self.sems.at[1, first + i],
                device_id=device, device_id_type=MESH,
            )
            for i, (src, dst, device) in enumerate(out)
        ]

    def start(self, stage):
        for copy in self.copies(stage):
            copy.start()

    def arrive(self, stage):
        for copy in self.copies(stage):
            copy.wait()

    def step(self, stage):
        last = 6 if self.scatter else 5
        if stage > last + 1:
            return
        if stage > 0:
            self.arrive(stage - 1)
        if stage == 1:
            mine = strip(coordinates()[3] * self.half, self.half)
            self.src[mine, :] = total_of([self.src[mine, :], self.rcore[...]])
        for part in range(3):
            if stage == 2:
                own = self.src[strip(self.home(part, 1), self.chunk), :]
                total = total_of([own] + [self.r1[part, i] for i in range(3)])
                self.w1[part] = total
                if not self.scatter:
                    self.r2[part, self.spot(part, 1)] = total
            elif stage == 3:
                if self.scatter:
                    own = self.w1[part, strip(self.spot(part, 1) * self.sub, self.sub), :]
                    total = total_of([own] + [self.r2[part, i] for i in range(3)])
                else:
                    total = total_of([self.r2[part, i] for i in range(4)])
                self.w2[part] = total
                self.r3[part, self.spot(part, 2)] = total
            elif stage == 4:
                here = strip(self.offset + self.home(part, 2), self.sub)
                self.fin[here, :] = total_of([self.r3[part, i] for i in range(4)])
        if stage <= last:
            self.start(stage)


EARLY = 10752
LATES = ((0, 1), (2,))
LATE = tuple(-(-(len(g) * 9 * LANES + 16) // 384) * 384 for g in LATES)


def main_kernel(
    tokens, cot, w_qkv, w_proj, w_expand, w_reduce,
    v_ag, v_as, v_qb, v_vb, v_pb, v_mg, v_ms, v_rb, v_eb, res, cnt,
    act_out, grad_out, early_out, late0_out, late1_out,
    x, up0, wq, wp, we, wr, n, nh, q, k, v, e0, e, bl, trio, a, ge, gh, gbl, hrecv, act_t,
    acc_d, acc_ff, lsem, osem, hsem, *rest,
):
    z = lax.axis_index("frame")
    sec, up, gb = trio.at[0], trio.at[1], trio.at[2]
    gj = trio
    jobs = [Sum(EARLY, True, ge, 0, *rest[:8]), Sum(LATE[0], False, ge, EARLY + PAIRS * 2 * F, *rest[8:16]), Sum(LATE[1], False, rest[16], 0, *rest[17:25])]
    early = jobs[0].src
    outs = [early_out, late0_out, late1_out]
    other = 1 - z

    def place(s):
        return s + z * (3 - 2 * s)

    local = []

    def fetch(src, dst):
        c = pltpu.make_async_copy(src, dst, lsem.at[len(local)])
        c.start()
        local.append(c)
        return c

    cx = [fetch(tokens.at[0, place(s)], x.at[s]) for s in range(N)]
    cq = [
        fetch(w_qkv.at[:, pl.ds((t * PAIRS + p) * LANES, LANES)], wq.at[:, pl.ds((p * 3 + t) * LANES, LANES)])
        for p in range(PAIRS) for t in range(3)
    ]
    enter()
    cp = fetch(w_proj, wp)
    ce = fetch(w_expand, we)
    cr = fetch(w_reduce, wr)
    cc = [fetch(cot.at[0, place(s)], up0.at[s]) for s in range(N)]

    attn_gain, attn_shift, query_bias, value_bias, proj_bias, mlp_gain, mlp_shift, reduce_bias, expand_bias = [
        ref[...].astype(f32).reshape(1, ref.shape[0])
        for ref in (v_ag, v_as, v_qb, v_vb, v_pb, v_mg, v_ms, v_rb, v_eb)
    ]

    def limit(s):
        frame = s + z * (7 - 2 * s)
        return jnp.where(frame < cnt[0], res[0], 0)

    for ref in (n, nh, sec, up, a, gb, *[q.at[p] for p in range(PAIRS)]):
        for s in range(ref.shape[0] // F):
            ref[pl.ds(s * F + T, F - T), :] = jnp.zeros((F - T, ref.shape[1]), ref.dtype)
    for p in range(PAIRS):
        for s in range(N):
            gbl[p, pl.ds(s * F + T, F - T), :] = jnp.zeros((F - T, LANES), bf16)
        for s in range(N + 1):
            k[p, pl.ds(s * F + T, F - T), :] = jnp.zeros((F - T, LANES), bf16)
            v[p, pl.ds(s * F + T, F - T), :] = jnp.zeros((F - T, LANES), bf16)
    for t in range(FF // LANES * N):
        ge[pl.ds(t * F + T, F - T), :] = jnp.zeros((F - T, LANES), bf16)
    row = lax.broadcasted_iota(jnp.int32, (F, LANES), 0)
    lane = lax.broadcasted_iota(jnp.int32, (F, LANES), 1)
    low = lane < 64

    def put_kv(s, p, keys, values):
        k[p, live_rows_of(s), :] = jnp.where(row[:T] < limit(s), keys, 0.0).astype(bf16)
        v[p, live_rows_of(s), :] = (values + value_bias[:, p * LANES:(p + 1) * LANES]).astype(bf16)

    for c in cx + cq:
        c.wait()

    def project(s, carry):
        scaled, _ = normalise(x[s].astype(f32))
        n[live_rows_of(s), :] = scaled.astype(bf16)
        joined = dot((scaled * attn_gain + attn_shift).astype(bf16), wq[...])
        for p in range(PAIRS):
            block = joined[:, p * D:(p + 1) * D]
            biased = (block[:, :LANES] + query_bias[:, p * LANES:(p + 1) * LANES]).astype(bf16)
            q[p, live_rows_of(s), :] = biased * jnp.asarray(0.125, bf16)
            put_kv(s, p, block[:, LANES:2 * LANES], block[:, 2 * LANES:])
        return carry

    lax.fori_loop(0, N, project, 0)

    entered()
    halo = pltpu.make_async_remote_copy(
        src_ref=tokens.at[0, place(N - 1)], dst_ref=x.at[N], send_sem=hsem.at[0], recv_sem=hsem.at[1],
        device_id={"frame": other}, device_id_type=MESH,
    )
    halo.start()

    def window(j):
        return list(range(max(j - 1, 0), j + 2))

    def span(j):
        w = window(j)
        return pl.ds(w[0] * F, len(w) * F)

    def bias_of(j):
        w = window(j)
        at = lax.broadcasted_iota(jnp.int32, (1, len(w) * F), 1)
        out = jnp.zeros((1, len(w) * F), f32)
        for i, s in enumerate(w):
            inside = (at >= i * F) & (at < (i + 1) * F)
            out = jnp.where(inside & (at >= i * F + limit(s)), NEG, out)
            out = jnp.where(inside & (at >= i * F + T), PAD, out)
        return out

    def half(value, h):
        zero = jnp.zeros_like(value)
        return jnp.where(low, value, zero) if h == 0 else jnp.where(low, zero, value)

    def values_at(p, j):
        return jnp.concatenate([v[p, span(j), :], jnp.ones((len(window(j)) * F, LANES), bf16)], axis=1)

    def weights_at(p, j, h):
        if j == 0:
            return e0.at[p, pl.ds(h * F, F)]
        return e.at[p * 3 + j - 1, pl.ds(h * F, F)]

    def forward(units):
        order = [(p, j, h) for p, j in units for h in range(2)]

        def scores(p, j, h):
            return dot(half(q[p, pl.ds(j * F, F), :], h), k[p, span(j), :], NT) + bias_of(j)

        s = scores(*order[0])
        held = []
        for i, (p, j, h) in enumerate(order):
            later = scores(*order[i + 1]) if i + 1 < len(order) else None
            largest = jnp.max(s, axis=1, keepdims=True)
            ex = jnp.exp(s - largest).astype(bf16)
            weights_at(p, j, h)[...] = ex
            o = dot(ex, values_at(p, j))
            total = o[:, LANES:]
            if j == 0:
                total = total + T * jnp.exp(NEG - largest)
            held.append((o[:, :LANES], 1.0 / total))
            if h == 1:
                (oa, ia), (ob, ib) = held
                held = []
                both = jnp.where(low, ia, ib)
                gh[j, :, pl.ds(pl.multiple_of(p * LANES, LANES), LANES)] = both[:T]
                bl[p, pl.ds(j * F, F), :] = (jnp.where(low, oa, ob) * both).astype(bf16)
            s = later

    def inner(p, carry):
        forward([(p, j) for j in range(N - 1)])
        return carry

    lax.fori_loop(0, PAIRS, inner, 0)
    halo.wait()
    scaled, _ = normalise(x[N].astype(f32))
    nh[pl.ds(0, T), :] = scaled.astype(bf16)
    normed = (scaled * attn_gain + attn_shift).astype(bf16)
    for p in range(PAIRS):
        block = dot(normed, wq[:, pl.ds(p * D + LANES, 2 * LANES)])
        put_kv(N, p, block[:, :LANES], block[:, LANES:])

    forward([(p, N - 1) for p in range(PAIRS)])


    for c in [cp, ce, cr] + cc:
        c.wait()
    acc_d[...] = jnp.zeros_like(acc_d)
    acc_ff[...] = jnp.zeros_like(acc_ff)
    live_row = lax.broadcasted_iota(jnp.int32, (T, D), 0)

    def hidden_of(j):
        blended = jnp.concatenate([bl[p, live_rows_of(j), :] for p in range(PAIRS)], axis=1)
        return x[j].astype(f32) + dot(blended, wp[...]) + proj_bias

    def mlp(i, carry):
        frames = [i * MLP_FRAMES + t for t in range(MLP_FRAMES)]
        units = [(t, c) for c in range(FF // CHUNK) for t in range(MLP_FRAMES)]
        state = []
        for j in frames:
            scaled, inverse = normalise(hidden_of(j))
            second = (scaled * mlp_gain + mlp_shift).astype(bf16)
            sec[live_rows_of(j), :] = second
            upstream = jnp.where(live_row < limit(j), up0[j].astype(f32), 0.0)
            up_low = upstream.astype(bf16)
            up[live_rows_of(j), :] = up_low
            acc_d[pl.ds(0, 1), :] += column_sum(upstream)
            state.append((scaled, inverse, second, upstream, up_low))

        def products(t, c):
            cols = pl.ds(c * CHUNK, CHUNK)
            return dot(state[t][2], we[:, cols]), dot(state[t][4], wr[cols, :], NT)

        now = products(*units[0])
        grad_second = [None] * MLP_FRAMES
        for at, (t, c) in enumerate(units):
            later = products(*units[at + 1]) if at + 1 < len(units) else None
            j = frames[t]
            cols = pl.ds(c * CHUNK, CHUNK)
            gelu, slope = gelu_parts(now[0] + expand_bias[:, c * CHUNK:(c + 1) * CHUNK])
            a[live_rows_of(j), cols] = gelu.astype(bf16)
            grad_low = (now[1] * slope).astype(bf16)
            for b in range(CHUNK // LANES):
                base = pl.multiple_of((c * (CHUNK // LANES) + b) * R + j * F, 16)
                ge[pl.ds(base, T), :] = grad_low[:, b * LANES:(b + 1) * LANES]
            acc_ff[:, cols] += column_sum(grad_low.astype(f32))
            part = dot(grad_low, we[:, cols], NT)
            grad_second[t] = part if grad_second[t] is None else grad_second[t] + part
            now = later
        for t, j in enumerate(frames):
            scaled, inverse, second, upstream, up_low = state[t]
            acc_d[pl.ds(1, 1), :] += column_sum(grad_second[t] * scaled)
            acc_d[pl.ds(2, 1), :] += column_sum(grad_second[t])
            grad_hidden = upstream + norm_back(grad_second[t], scaled, inverse, mlp_gain)
            branch = grad_hidden.astype(bf16)
            gb[live_rows_of(j), :] = branch
            acc_d[pl.ds(3, 1), :] += column_sum(branch.astype(f32))
            grad_blended = (dot(branch, wp[...], NT).astype(bf16).astype(f32) * gh[j]).astype(bf16)
            gh[j] = grad_hidden
            for p in range(PAIRS):
                gbl[p, live_rows_of(j), :] = grad_blended[:, p * LANES:(p + 1) * LANES]
        return carry

    lax.fori_loop(0, N // MLP_FRAMES, mlp, 0)

    def pack(ref, base, block):
        block = block.astype(bf16)
        for t in range(block.shape[1] // LANES):
            ref[pl.ds(base + t * D, D), :] = block[:, t * LANES:(t + 1) * LANES]

    def pack_vectors(ref, base, rows, vectors):
        pieces = [w[:, t * LANES:(t + 1) * LANES] for w in vectors for t in range(w.shape[1] // LANES)]
        pieces.append(jnp.zeros((rows - len(pieces), LANES), f32))
        ref[pl.ds(base, rows), :] = jnp.concatenate(pieces, axis=0).astype(bf16)

    def big_weights(c, carry):
        cols = pl.ds(pl.multiple_of(c * D, LANES), D)
        base = pl.multiple_of(c * 3 * D, 16)
        pack(early, base, dot(sec[...], jnp.concatenate([ge[pl.ds(pl.multiple_of((c * 3 + t) * R, 16), R), :] for t in range(3)], axis=1), TN))
        pack(early, base + 12 * D, dot(up[...], a[:, cols], TN))
        return carry

    lax.fori_loop(0, FF // D, big_weights, 0)
    blended = jnp.concatenate([bl[p] for p in range(PAIRS)], axis=1)
    pack(early, 24 * D, dot(blended, gb[...], TN))
    pack_vectors(
        early, 27 * D, EARLY - 27 * D,
        [acc_d[pl.ds(0, 1), :], acc_ff[...], acc_d[pl.ds(1, 1), :], acc_d[pl.ds(2, 1), :], acc_d[pl.ds(3, 1), :]],
    )
    jobs[0].step(0)

    sums_ref = acc_d

    def lanes_of(i):
        return pl.ds(pl.multiple_of(i * LANES, LANES), LANES)

    def cols_of(p):
        return pl.ds(pl.multiple_of(p * D, LANES), D)

    def edge_rows(p, t):
        return pl.ds(pl.multiple_of(EARLY + p * 2 * F + t * F, 16), F)

    def edge(p):
        return pltpu.make_async_remote_copy(
            src_ref=ge.at[pl.ds(pl.multiple_of(EARLY + p * 2 * F, 16), 2 * F), :], dst_ref=hrecv.at[p], send_sem=hsem.at[2 + p],
            recv_sem=hsem.at[5 + p], device_id={"frame": other}, device_id_type=MESH,
        )

    def backward(p, carry):
        order = [(j, h) for j in (3, 2, 1, 0) for h in range(2)]
        prepared = {}

        def prepare(j):
            at = pl.ds(j * F, F)
            g = gbl[p, at, :]
            product = g.astype(f32) * (-bl[p, at, :].astype(f32))
            high = product.astype(bf16)
            rest = pltpu.roll(product - high.astype(f32), 64, 1).astype(bf16)
            return g, high, rest

        def grad_weights(j, h):
            if j not in prepared:
                prepared[j] = prepare(j)
            g, high, rest = prepared[j]
            extra = jnp.where(low, high, rest) if h == 0 else jnp.where(low, rest, high)
            return dot(jnp.concatenate([half(g, h), extra], axis=1), values_at(p, j), NT)

        sums = {}

        def add(s, part):
            sums[s] = part if s not in sums else [y + w for y, w in zip(sums[s], part)]

        dp = grad_weights(*order[0])
        scores = []
        queries = []
        for i, (j, h) in enumerate(order):
            later = grad_weights(*order[i + 1]) if i + 1 < len(order) else None
            ds = (dp * weights_at(p, j, h)[...].astype(f32)).astype(bf16)
            scores.append(ds)
            queries.append(dot(ds, k[p, span(j), :]))
            if h == 1:
                at = pl.ds(j * F, F)
                gj[p, at, pl.ds(0, LANES)] = (jnp.where(low, queries[0], queries[1]) * 0.125).astype(bf16)
                qq = q[p, at, :]
                g = prepared[j][0]
                dk = dot(
                    jnp.concatenate([half(qq, 0), half(qq, 1)], axis=0), jnp.concatenate(scores, axis=0), TN
                ).T
                both = e0[p] if j == 0 else e[p * 3 + j - 1]
                dv = dot(jnp.concatenate([half(g, 0), half(g, 1)], axis=0), both, TN).T
                for t, s in enumerate(window(j)):
                    add(s, [dk[t * F:(t + 1) * F], dv[t * F:(t + 1) * F]])
                scores, queries = [], []
                if j == 3:
                    ge[edge_rows(p, 0), :] = sums[N][0].astype(bf16)
                    ge[edge_rows(p, 1), :] = sums[N][1].astype(bf16)
                    edge(p).start()
            dp = later
        for s in range(N):
            for t in range(2):
                gj[p, pl.ds(s * F, F), pl.ds((1 + t) * LANES, LANES)] = sums[s][t].astype(bf16)
        columns = gj[p]
        outer = jnp.concatenate([ge[edge_rows(p, t), :] for t in range(2)], axis=1)
        outer_moment = dot(nh[...], outer, TN)
        moment = dot(n[...], columns, TN)
        moment = jnp.concatenate([moment[:, :LANES], moment[:, LANES:] + outer_moment], axis=1)
        summed = column_sum(columns.astype(f32))
        outer_sum = column_sum(outer.astype(f32))
        summed = jnp.concatenate([summed[:, :LANES], summed[:, LANES:] + outer_sum], axis=1)

        def put(group, first):
            job = jobs[1 + group]
            pack(job.src, pl.multiple_of((p - first) * 3 * D, 16), moment)
            sums_ref[pl.ds(p, 1), :] = summed

        def send(group):
            pairs = LATES[group]
            base = len(pairs) * 3 * D
            pack_vectors(jobs[1 + group].src, base, LATE[group] - base, [sums_ref[pl.ds(i, 1), :] for i in pairs])
            jobs[1 + group].step(0)

        @pl.when(p == 0)
        def _():
            put(0, 0)

        @pl.when(p == 1)
        def _():
            put(0, 0)
            send(0)

        @pl.when(p == 2)
        def _():
            put(1, 2)
            send(1)
            jobs[1].step(1)

        for i in range(PAIRS):
            @pl.when(p == i)
            def _():
                jobs[0].step(i + 1)

        return carry

    lax.fori_loop(0, PAIRS, backward, 0)

    def settle():
        for p in range(PAIRS):
            edge(p).wait()
            for t in range(2):
                at, cols = pl.ds(3 * F, F), pl.ds((1 + t) * LANES, LANES)
                gj[p, at, cols] = (gj[p, at, cols].astype(f32) + hrecv[p, pl.ds(t * F, F), :].astype(f32)).astype(bf16)

    def tail(finish):
        E, A, B = jobs
        finish(0, 0)
        B.step(1)
        finish(1, 0)
        A.step(2)
        E.step(4)
        finish(2, 0)
        B.step(2)
        settle()
        finish(3, 0)
        A.step(3)
        E.step(5)
        output(0)
        output(1)
        B.step(3)
        output(2)
        output(3)
        A.step(4)
        ordered = jnp.stack([up0[place(i)] for i in range(N)], axis=0)
        act_t[...] = jnp.swapaxes(ordered, 0, 1)
        pltpu.make_async_copy(act_t, act_out.at[0], osem.at[0]).start()
        B.step(4)
        E.step(6)
        A.step(5)
        B.step(5)
        A.step(6)
        E.step(7)
        B.step(6)

    def output(j):
        out = hidden_of(j) + dot(a[live_rows_of(j), :], wr[...]) + reduce_bias
        up0[j] = out.astype(bf16)

    def finish(j, carry):
        grad_normed = dot(jnp.concatenate([gj[p, live_rows_of(j), :] for p in range(PAIRS)], axis=1), wq[...], NT)
        scaled, inverse = normalise(x[j].astype(f32))
        gh[j] = gh[j] + norm_back(grad_normed, scaled, inverse, attn_gain)
        pltpu.make_async_copy(gh.at[j], grad_out.at[0, :, place(j), :], osem.at[4 + j]).start()
        return carry

    tail(finish)
    for i, job in enumerate(jobs):
        copy = pltpu.make_async_copy(job.fin.at[pl.ds(job.offset, job.rows)], outs[i], osem.at[8 + i])
        copy.start()
    for j in range(N):
        pltpu.make_async_copy(gh.at[j], grad_out.at[0, :, place(j), :], osem.at[4 + j]).wait()
    pltpu.make_async_copy(act_t, act_out.at[0], osem.at[0]).wait()
    for i, job in enumerate(jobs):
        pltpu.make_async_copy(job.fin.at[pl.ds(job.offset, job.rows)], outs[i], osem.at[8 + i]).wait()


def run_main(tokens, cot, w_qkv, w_proj, w_expand, w_reduce, *rest):
    hbm = pl.BlockSpec(memory_space=pl.ANY)
    vmem = pl.BlockSpec(memory_space=pltpu.VMEM)
    smem = pl.BlockSpec(memory_space=pltpu.SMEM)
    V = pltpu.VMEM
    scratch = [
        V((N + 1, T, D), bf16), V((N, T, D), bf16), V((D, 3 * D), bf16), V((D, D), bf16), V((D, FF), bf16), V((FF, D), bf16),
        V((R, D), bf16), V((F, D), bf16), V((PAIRS, R, LANES), bf16), V((PAIRS, R + F, LANES), bf16), V((PAIRS, R + F, LANES), bf16),
        V((PAIRS, 2 * F, 2 * F), bf16), V((PAIRS * 3, 2 * F, 3 * F), bf16),
        V((PAIRS, R, LANES), bf16),
        V((3, R, D), bf16), V((R, FF), bf16), V((FF // LANES * R, LANES), bf16), V((N, T, D), f32),
        V((PAIRS, R, LANES), bf16),
        V((PAIRS, 2 * F, LANES), bf16), V((T, N, D), bf16), V((8, D), f32), V((1, FF), f32),
        pltpu.SemaphoreType.DMA((24,)), pltpu.SemaphoreType.DMA((11,)), pltpu.SemaphoreType.DMA((8,)),
    ] + Sum.scratch(EARLY, True) + Sum.scratch(LATE[0], False) + [V((LATE[1], LANES), bf16)] + Sum.scratch(LATE[1], False)
    return pl.pallas_call(
        main_kernel,
        out_shape=[
            jax.ShapeDtypeStruct((1, T, N, D), bf16), jax.ShapeDtypeStruct((1, T, N, D), f32),
            jax.ShapeDtypeStruct((EARLY, LANES), bf16), jax.ShapeDtypeStruct((LATE[0], LANES), bf16),
            jax.ShapeDtypeStruct((LATE[1], LANES), bf16),
        ],
        in_specs=[hbm] * 6 + [vmem] * 9 + [smem] * 2,
        out_specs=[hbm] * 5,
        scratch_shapes=scratch,
        compiler_params=pltpu.CompilerParams(
            collective_id=0, has_side_effects=True, vmem_limit_bytes=66_500_000
        ),
    )(tokens, cot, w_qkv, w_proj, w_expand, w_reduce, *rest)


def final_kernel(
    early_in, late0_in, late1_in, wq_in, gain_ref, shift_ref, act_in, grad_in,
    o_ag, o_as, o_wq, o_qb, o_vb, o_wp, o_pb, o_mg, o_ms, o_we, o_eb, o_wr, o_rb, o_norm, o_act, o_grad,
    early, late0, late1, wq, s_wq, s_wp, s_we, s_wr, s_act, s_grad, isem, osem,
):
    half = 12 * D
    pieces = [
        (early_in.at[pl.ds(half, half)], early.at[pl.ds(half, half)]), (early_in.at[pl.ds(0, half)], early.at[pl.ds(0, half)]),
        (early_in.at[pl.ds(2 * half, EARLY - 2 * half)], early.at[pl.ds(2 * half, EARLY - 2 * half)]),
        (late0_in, late0), (late1_in, late1), (wq_in, wq),
    ]
    fetches = [pltpu.make_async_copy(src, dst, isem.at[i]) for i, (src, dst) in enumerate(pieces)]
    for copy in fetches:
        copy.start()

    whole = [pltpu.make_async_copy(act_in, s_act, isem.at[6]), pltpu.make_async_copy(grad_in, s_grad, isem.at[7])]
    for copy in whole:
        copy.start()

    def square(total, block):
        return total + jnp.sum(block * block, axis=0, keepdims=True)

    total = jnp.zeros((1, LANES), f32)
    stores = []

    def store(src, dst):
        copy = pltpu.make_async_copy(src, dst, osem.at[len(stores)])
        copy.start()
        stores.append(copy)

    fetches[0].wait()
    for c in range(12):
        block = early[pl.ds(half + c * D, D), :].astype(f32)
        s_wr[pl.ds(c * LANES, LANES), :] = block.T
        total = square(total, block)
    store(s_wr, o_wr)
    whole[0].wait()
    store(s_act, o_act)
    whole[1].wait()
    store(s_grad, o_grad)
    fetches[1].wait()
    for c in range(12):
        block = early[pl.ds(c * D, D), :].astype(f32)
        s_we[:, pl.ds(c * LANES, LANES)] = block
        total = square(total, block)
    store(s_we, o_we)
    fetches[2].wait()
    for c in range(3):
        block = early[pl.ds(2 * half + c * D, D), :].astype(f32)
        s_wp[:, pl.ds(c * LANES, LANES)] = block
        total = square(total, block)
    store(s_wp, o_wp)
    tail = early[pl.ds(27 * D, 32), :].astype(f32)
    total = square(total, tail[:24])
    lines = [tail[i:i + 1] for i in range(24)]

    def line(parts):
        return jnp.concatenate(parts, axis=1).reshape(len(parts) * LANES)

    o_rb[...] = line(lines[:3])
    o_eb[...] = line(lines[3:15])
    o_mg[...] = line(lines[15:18])
    o_ms[...] = line(lines[18:21])
    o_pb[...] = line(lines[21:24])

    def column(ref):
        row = ref[...].reshape(1, D)
        return jnp.broadcast_to(row, (LANES, D)).T

    gain, shift = column(gain_ref), column(shift_ref)
    for copy in fetches[3:]:
        copy.wait()
    along_gain = jnp.zeros((D, LANES), f32)
    along_shift = jnp.zeros((D, LANES), f32)
    sums = {}
    for group, ref in ((0, late0), (1, late1)):
        pairs = LATES[group]
        extra = ref[pl.ds(len(pairs) * 3 * D, 16), :].astype(f32)
        for i, p in enumerate(pairs):
            for t in range(3):
                moment = ref[pl.ds((i * 3 + t) * D, D), :].astype(f32)
                summed = extra[i * 3 + t:i * 3 + t + 1]
                sums[t, p] = summed
                cols = pl.ds((t * PAIRS + p) * LANES, LANES)
                weight = wq[:, cols].astype(f32)
                block = gain * moment + shift * summed
                s_wq[:, cols] = block
                total = square(total, block)
                along_gain = along_gain + weight * moment
                along_shift = along_shift + weight * summed
    store(s_wq, o_wq)
    grad_gain = jnp.sum(along_gain.T, axis=0, keepdims=True)
    grad_shift = jnp.sum(along_shift.T, axis=0, keepdims=True)
    o_ag[...] = grad_gain.reshape(D)
    o_as[...] = grad_shift.reshape(D)
    o_qb[...] = line([sums[0, p] for p in range(PAIRS)])
    o_vb[...] = line([sums[2, p] for p in range(PAIRS)])
    for p in range(PAIRS):
        total = square(square(total, sums[0, p]), sums[2, p])
        cols = slice(p * LANES, (p + 1) * LANES)
        total = square(square(total, grad_gain[:, cols]), grad_shift[:, cols])
    o_norm[...] = jnp.sqrt(jnp.sum(total, axis=1, keepdims=True))
    for copy in stores:
        copy.wait()


def run_final(early, late0, late1, w_qkv, gain, shift, act, grad):
    hbm = pl.BlockSpec(memory_space=pl.ANY)
    vmem = pl.BlockSpec(memory_space=pltpu.VMEM)
    V = pltpu.VMEM
    vector = jax.ShapeDtypeStruct((D,), f32)

    def matrix(a, b):
        return jax.ShapeDtypeStruct((a, b), f32)

    shapes = [
        vector, vector, matrix(D, 3 * D), vector, vector, matrix(D, D), vector, vector, vector, matrix(D, FF),
        jax.ShapeDtypeStruct((FF,), f32), matrix(FF, D), vector, matrix(1, 1),
        jax.ShapeDtypeStruct(act.shape, act.dtype), jax.ShapeDtypeStruct(grad.shape, grad.dtype),
    ]
    return pl.pallas_call(
        final_kernel,
        out_shape=shapes,
        in_specs=[hbm] * 4 + [vmem] * 2 + [hbm] * 2,
        out_specs=[hbm if len(s.shape) > 1 and s.shape[-1] > 1 else vmem for s in shapes],
        scratch_shapes=[
            V((EARLY, LANES), bf16), V((LATE[0], LANES), bf16), V((LATE[1], LANES), bf16), V((D, 3 * D), bf16),
            V((D, 3 * D), f32), V((D, D), f32), V((D, FF), f32), V((FF, D), f32),
            V(act.shape, bf16), V(grad.shape, f32),
            pltpu.SemaphoreType.DMA((8,)), pltpu.SemaphoreType.DMA((6,)),
        ],
        compiler_params=pltpu.CompilerParams(vmem_limit_bytes=66_500_000),
    )(early, late0, late1, w_qkv, gain, shift, act, grad)


def body(
    tokens, attn_gain, attn_shift, w_qkv, query_bias, value_bias, w_proj, proj_bias, mlp_gain, mlp_shift,
    w_expand, expand_bias, w_reduce, reduce_bias, cotangent, resolution, frame_count,
):
    act, grad, early, late0, late1 = run_main(
        tokens, cotangent, w_qkv, w_proj, w_expand, w_reduce, attn_gain, attn_shift, query_bias, value_bias,
        proj_bias, mlp_gain, mlp_shift, reduce_bias, expand_bias, resolution, frame_count,
    )
    *grads, norm, act, grad = run_final(early, late0, late1, w_qkv, attn_gain, attn_shift, act, grad)
    return (jnp.transpose(act, (0, 2, 1, 3)), jnp.transpose(grad, (0, 2, 1, 3)), *grads, norm.reshape(()))


def solution(mesh):
    data = P("clip", "frame", None, None)
    return jax.shard_map(
        body,
        mesh=mesh,
        in_specs=(data,) + (P(),) * 13 + (data, P("clip"), P("clip")),
        out_specs=(data, data) + (P(),) * 14,
        check_vma=False,
    )
```

time: 123 us -> 110 us (0.89)
  Pallas kernels: 111 us -> 104 us
  local copies, waits for them, and re-layouts: 9.13 us -> 3.37 us
    pallas_call x1, Pallas kernels: 106 us -> 95.7 us  [run_main(): pl.pallas_call(main_kernel, out_shape=[jax.ShapeDtypeStruct((1, T, N, D),...]
    unnamed x20 -> x4, local copies, waits for them, and re-layouts: 9.13 us -> 3.37 us
    pallas_call x1, Pallas kernels: 5.53 us -> 8.75 us  [run_final(): pl.pallas_call(final_kernel, out_shape=shapes, in_specs=[hbm] * 4 + [vmem...]
where the time goes in v3:
time: 110 us
  Pallas kernels  104 us (95%)
  local copies, waits for them, and re-layouts  3.37 us (3%)
  between operations  2.24 us (2%)
    pallas_call x1, Pallas kernels, run_main(): pl.pallas_call(main_kernel, out_shape=[jax.ShapeDtypeStruct((1, T, N, D),...  95.7 us
    pallas_call x1, Pallas kernels, run_final(): pl.pallas_call(final_kernel, out_shape=shapes, in_specs=[hbm] * 4 + [vmem...  8.75 us
    unnamed x4, local copies, waits for them, and re-layouts  3.37 us

profile of v3, /device:TPU:1, one launch (start us, length us, event | category | flops | bytes accessed | tf_op | source)
XLA Modules:
  0.0 110.1 jit_solution(11332753302554440897)
XLA Ops:
  0.6 0.0 copy-start
  2.0 2.3 %copy.33.tokens = bf16[1,4,324,384]{3,2,1,0:T(8,128)(2,1)} copy(bf16[1,4,324,384]{3,1,2,0:T(4,128)(2,1)} %param.17) | data formatting | bytes 1990656 | tf_op args[0]
  4.3 0.0 copy-done
  4.3 1.1 copy.34.cot
  5.4 95.7 %shard_map.288 = (bf16[1,324,4,384]{3,2,1,0:T(4,128)(2,1)}, f32[1,324,4,384]{3,2,1,0:T(4,128)}, bf16[10752,128]{1,0:T(8,128)(2,1)}, bf16[2688,128]{1,0:T(8,128)(2,1)}, bf16[1536,128]{1,0:T(8,128)(2,1)}) custom-call(bf16[1,4,324,384]{3,2,1,0:T(8,128)(2,1)} %copy.33.tokens, bf16[1,4,324,384]{3,2,1,0:T(8,128)(2,1)} %copy.34.cot, bf16[384,1152]{1,0:T(8,128)(2,1)} %wq_in.1, ...), custom_call_target="tpu_custom_call" | custom-call | tf_op jit(solution)/shard_map/pallas_call | solution.py:664
  101.2 8.8 %shard_map.289 = (f32[384]{0:T(512)}, f32[384]{0:T(512)}, f32[384,1152]{1,0:T(8,128)}, f32[384]{0:T(512)}, f32[384]{0:T(512)}, /*index=5*/f32[384,384]{1,0:T(8,1...) custom-call(bf16[10752,128]{1,0:T(8,128)(2,1)} %get-tuple-element.37, ...), custom_call_target="tpu_custom_call" | custom-call | tf_op jit(solution)/shard_map/pallas_call | solution.py:800
Async XLA Ops:
  0.6 3.7 %copy-start = (bf16[1,4,324,384]{3,1,2,0:T(4,128)(2,1)S(1)}, bf16[1,4,324,384]{3,1,2,0:T(4,128)(2,1)}, u32[]{:S(2)}) copy-start(bf16[1,4,324,384]{3,1,2,0:T(4,128)(2,1)} %param.31) | copy-start | bytes 2985988

commit v4 on v3

--- a/solution.py
+++ b/solution.py
@@ -223,6 +223,8 @@
             self.start(stage)
 
 
+FIRST = 4608
+SECOND = 6144
 EARLY = 10752
 LATES = ((0, 1), (2,))
 LATE = tuple(-(-(len(g) * 9 * LANES + 16) // 384) * 384 for g in LATES)
@@ -238,9 +240,9 @@
     z = lax.axis_index("frame")
     sec, up, gb = trio.at[0], trio.at[1], trio.at[2]
     gj = trio
-    jobs = [Sum(EARLY, True, ge, 0, *rest[:8]), Sum(LATE[0], False, ge, EARLY + PAIRS * 2 * F, *rest[8:16]), Sum(LATE[1], False, rest[16], 0, *rest[17:25])]
-    early = jobs[0].src
-    outs = [early_out, late0_out, late1_out]
+    jobs = [Sum(FIRST, True, ge, 0, *rest[:8]), Sum(LATE[0], False, ge, EARLY + PAIRS * 2 * F, *rest[8:16]), Sum(LATE[1], False, rest[16], 0, *rest[17:25]),
+            Sum(SECOND, True, ge, FIRST, *rest[25:33])]
+    outs = [early_out.at[pl.ds(0, FIRST)], late0_out, late1_out, early_out.at[pl.ds(FIRST, SECOND)]]
     other = 1 - z
 
     def place(s):
@@ -457,21 +459,30 @@
         pieces.append(jnp.zeros((rows - len(pieces), LANES), f32))
         ref[pl.ds(base, rows), :] = jnp.concatenate(pieces, axis=0).astype(bf16)
 
-    def big_weights(c, carry):
+    first, second_job = jobs[0], jobs[3]
+
+    def reduce_weights(c, carry):
         cols = pl.ds(pl.multiple_of(c * D, LANES), D)
-        base = pl.multiple_of(c * 3 * D, 16)
-        pack(early, base, dot(sec[...], jnp.concatenate([ge[pl.ds(pl.multiple_of((c * 3 + t) * R, 16), R), :] for t in range(3)], axis=1), TN))
-        pack(early, base + 12 * D, dot(up[...], a[:, cols], TN))
+        pack(first.src, pl.multiple_of(c * 3 * D, 16), dot(up[...], a[:, cols], TN))
         return carry
 
-    lax.fori_loop(0, FF // D, big_weights, 0)
+    lax.fori_loop(0, FF // D, reduce_weights, 0)
+    first.step(0)
+
+    def expand_weights(c, carry):
+        tiles = [ge[pl.ds(pl.multiple_of((c * 3 + t) * R, 16), R), :] for t in range(3)]
+        pack(second_job.src, pl.multiple_of(c * 3 * D, 16), dot(sec[...], jnp.concatenate(tiles, axis=1), TN))
+        return carry
+
+    lax.fori_loop(0, FF // D, expand_weights, 0)
     blended = jnp.concatenate([bl[p] for p in range(PAIRS)], axis=1)
-    pack(early, 24 * D, dot(blended, gb[...], TN))
+    pack(second_job.src, 12 * D, dot(blended, gb[...], TN))
     pack_vectors(
-        early, 27 * D, EARLY - 27 * D,
+        second_job.src, 15 * D, SECOND - 15 * D,
         [acc_d[pl.ds(0, 1), :], acc_ff[...], acc_d[pl.ds(1, 1), :], acc_d[pl.ds(2, 1), :], acc_d[pl.ds(3, 1), :]],
     )
-    jobs[0].step(0)
+    first.step(1)
+    second_job.step(0)
 
     sums_ref = acc_d
 
@@ -489,6 +500,13 @@
             src_ref=ge.at[pl.ds(pl.multiple_of(EARLY + p * 2 * F, 16), 2 * F), :], dst_ref=hrecv.at[p], send_sem=hsem.at[2 + p],
             recv_sem=hsem.at[5 + p], device_id={"frame": other}, device_id_type=MESH,
         )
+
+    def advance(p, sites):
+        for i in range(PAIRS):
+            @pl.when(p == i)
+            def _():
+                for job, stage in sites[i]:
+                    job.step(stage)
 
     def backward(p, carry):
         order = [(j, h) for j in (3, 2, 1, 0) for h in range(2)]
@@ -539,6 +557,8 @@
                     ge[edge_rows(p, 0), :] = sums[N][0].astype(bf16)
                     ge[edge_rows(p, 1), :] = sums[N][1].astype(bf16)
                     edge(p).start()
+                if j == 2:
+                    advance(p, [[(second_job, 1)], [(second_job, 2)], [(second_job, 3), (first, 4)]])
             dp = later
         for s in range(N):
             for t in range(2):
@@ -578,10 +598,7 @@
             send(1)
             jobs[1].step(1)
 
-        for i in range(PAIRS):
-            @pl.when(p == i)
-            def _():
-                jobs[0].step(i + 1)
+        advance(p, [[(first, 2)], [(first, 3)], [(second_job, 4), (first, 5)]])
 
         return carry
 
@@ -595,34 +612,46 @@
                 gj[p, at, cols] = (gj[p, at, cols].astype(f32) + hrecv[p, pl.ds(t * F, F), :].astype(f32)).astype(bf16)
 
     def tail(finish):
-        E, A, B = jobs
+        E, A, B, G = jobs
         finish(0, 0)
         B.step(1)
         finish(1, 0)
         A.step(2)
-        E.step(4)
         finish(2, 0)
+        settle()
+        G.step(5)
         B.step(2)
-        settle()
         finish(3, 0)
+        E.step(6)
+        output(0)
         A.step(3)
-        E.step(5)
-        output(0)
         output(1)
+        output(2)
         B.step(3)
-        output(2)
         output(3)
         A.step(4)
+        E.step(7)
+        leave(0)
+        G.step(6)
+        B.step(4)
         ordered = jnp.stack([up0[place(i)] for i in range(N)], axis=0)
         act_t[...] = jnp.swapaxes(ordered, 0, 1)
         pltpu.make_async_copy(act_t, act_out.at[0], osem.at[0]).start()
-        B.step(4)
-        E.step(6)
         A.step(5)
+        G.step(7)
+        leave(3)
         B.step(5)
         A.step(6)
-        E.step(7)
+        leave(1)
         B.step(6)
+        leave(2)
+
+    def result(i):
+        job = jobs[i]
+        return pltpu.make_async_copy(job.fin.at[pl.ds(job.offset, job.rows)], outs[i], osem.at[8 + i])
+
+    def leave(i):
+        result(i).start()
 
     def output(j):
         out = hidden_of(j) + dot(a[live_rows_of(j), :], wr[...]) + reduce_bias
@@ -636,14 +665,11 @@
         return carry
 
     tail(finish)
-    for i, job in enumerate(jobs):
-        copy = pltpu.make_async_copy(job.fin.at[pl.ds(job.offset, job.rows)], outs[i], osem.at[8 + i])
-        copy.start()
     for j in range(N):
         pltpu.make_async_copy(gh.at[j], grad_out.at[0, :, place(j), :], osem.at[4 + j]).wait()
     pltpu.make_async_copy(act_t, act_out.at[0], osem.at[0]).wait()
-    for i, job in enumerate(jobs):
-        pltpu.make_async_copy(job.fin.at[pl.ds(job.offset, job.rows)], outs[i], osem.at[8 + i]).wait()
+    for i in range(len(jobs)):
+        result(i).wait()
 
 
 def run_main(tokens, cot, w_qkv, w_proj, w_expand, w_reduce, *rest):
@@ -659,8 +685,8 @@
         V((3, R, D), bf16), V((R, FF), bf16), V((FF // LANES * R, LANES), bf16), V((N, T, D), f32),
         V((PAIRS, R, LANES), bf16),
         V((PAIRS, 2 * F, LANES), bf16), V((T, N, D), bf16), V((8, D), f32), V((1, FF), f32),
-        pltpu.SemaphoreType.DMA((24,)), pltpu.SemaphoreType.DMA((11,)), pltpu.SemaphoreType.DMA((8,)),
-    ] + Sum.scratch(EARLY, True) + Sum.scratch(LATE[0], False) + [V((LATE[1], LANES), bf16)] + Sum.scratch(LATE[1], False)
+        pltpu.SemaphoreType.DMA((24,)), pltpu.SemaphoreType.DMA((12,)), pltpu.SemaphoreType.DMA((8,)),
+    ] + Sum.scratch(FIRST, True) + Sum.scratch(LATE[0], False) + [V((LATE[1], LANES), bf16)] + Sum.scratch(LATE[1], False) + Sum.scratch(SECOND, True)
     return pl.pallas_call(
         main_kernel,
         out_shape=[
@@ -684,16 +710,15 @@
 ):
     half = 12 * D
     pieces = [
-        (early_in.at[pl.ds(half, half)], early.at[pl.ds(half, half)]), (early_in.at[pl.ds(0, half)], early.at[pl.ds(0, half)]),
+        (early_in.at[pl.ds(0, half)], early.at[pl.ds(0, half)]), (early_in.at[pl.ds(half, half)], early.at[pl.ds(half, half)]),
         (early_in.at[pl.ds(2 * half, EARLY - 2 * half)], early.at[pl.ds(2 * half, EARLY - 2 * half)]),
         (late0_in, late0), (late1_in, late1), (wq_in, wq),
     ]
+    whole = [pltpu.make_async_copy(act_in, s_act, isem.at[6]), pltpu.make_async_copy(grad_in, s_grad, isem.at[7])]
+    for copy in whole:
+        copy.start()
     fetches = [pltpu.make_async_copy(src, dst, isem.at[i]) for i, (src, dst) in enumerate(pieces)]
     for copy in fetches:
-        copy.start()
-
-    whole = [pltpu.make_async_copy(act_in, s_act, isem.at[6]), pltpu.make_async_copy(grad_in, s_grad, isem.at[7])]
-    for copy in whole:
         copy.start()
 
     def square(total, block):
@@ -707,19 +732,19 @@
         copy.start()
         stores.append(copy)
 
-    fetches[0].wait()
-    for c in range(12):
-        block = early[pl.ds(half + c * D, D), :].astype(f32)
-        s_wr[pl.ds(c * LANES, LANES), :] = block.T
-        total = square(total, block)
-    store(s_wr, o_wr)
     whole[0].wait()
     store(s_act, o_act)
     whole[1].wait()
     store(s_grad, o_grad)
+    fetches[0].wait()
+    for c in range(12):
+        block = early[pl.ds(c * D, D), :].astype(f32)
+        s_wr[pl.ds(c * LANES, LANES), :] = block.T
+        total = square(total, block)
+    store(s_wr, o_wr)
     fetches[1].wait()
     for c in range(12):
-        block = early[pl.ds(c * D, D), :].astype(f32)
+        block = early[pl.ds(half + c * D, D), :].astype(f32)
         s_we[:, pl.ds(c * LANES, LANES)] = block
         total = square(total, block)
     store(s_we, o_we)

time: 110 us -> 110 us (level)
  no operation moved by 1% of the time
where the time goes in v4:
time: 110 us; the launch traced here: 109 us
  Pallas kernels  104 us (95%)
  local copies, waits for them, and re-layouts  3.37 us (3%)
  between operations  2.24 us (2%)
    pallas_call x1, Pallas kernels, run_main(): pl.pallas_call(main_kernel, out_shape=[jax.ShapeDtypeStruct((1, T, N, D),...  95.2 us
    pallas_call x1, Pallas kernels, run_final(): pl.pallas_call(final_kernel, out_shape=shapes, in_specs=[hbm] * 4 + [vmem...  8.71 us
    unnamed x4, local copies, waits for them, and re-layouts  3.37 us

profile of v4, /device:TPU:1, one launch (start us, length us, event | category | flops | bytes accessed | tf_op | source)
XLA Modules:
  0.0 109.5 jit_solution(6687324656919386008)
XLA Ops:
  0.6 0.0 copy-start
  2.0 2.3 %copy.33.tokens = bf16[1,4,324,384]{3,2,1,0:T(8,128)(2,1)} copy(bf16[1,4,324,384]{3,1,2,0:T(4,128)(2,1)} %param.17) | data formatting | bytes 1990656 | tf_op args[0]
  4.3 0.0 copy-done
  4.3 1.1 copy.34.cot
  5.4 95.2 %shard_map.288 = (bf16[1,324,4,384]{3,2,1,0:T(4,128)(2,1)}, f32[1,324,4,384]{3,2,1,0:T(4,128)}, bf16[10752,128]{1,0:T(8,128)(2,1)}, bf16[2688,128]{1,0:T(8,128)(2,1)}, bf16[1536,128]{1,0:T(8,128)(2,1)}) custom-call(bf16[1,4,324,384]{3,2,1,0:T(8,128)(2,1)} %copy.33.tokens, bf16[1,4,324,384]{3,2,1,0:T(8,128)(2,1)} %copy.34.cot, bf16[384,1152]{1,0:T(8,128)(2,1)} %wq_in.1, ...), custom_call_target="tpu_custom_call" | custom-call | tf_op jit(solution)/shard_map/pallas_call | solution.py:690
  100.6 8.7 %shard_map.289 = (f32[384]{0:T(512)}, f32[384]{0:T(512)}, f32[384,1152]{1,0:T(8,128)}, f32[384]{0:T(512)}, f32[384]{0:T(512)}, /*index=5*/f32[384,384]{1,0:T(8,1...) custom-call(bf16[10752,128]{1,0:T(8,128)(2,1)} %get-tuple-element.37, ...), custom_call_target="tpu_custom_call" | custom-call | tf_op jit(solution)/shard_map/pallas_call | solution.py:825
Async XLA Ops:
  0.6 3.7 %copy-start = (bf16[1,4,324,384]{3,1,2,0:T(4,128)(2,1)S(1)}, bf16[1,4,324,384]{3,1,2,0:T(4,128)(2,1)}, u32[]{:S(2)}) copy-start(bf16[1,4,324,384]{3,1,2,0:T(4,128)(2,1)} %param.31) | copy-start | bytes 2985988
